TPU v7x, 512 devices: a whole 4x8x8 slice. The times are simulated.
512 devices in a mesh: dp: 4 (over y_hi), ctx: 16 (over x, y_lo, core), tp: 8 (over z).
Axes of the slice: x: 4, y: 8 (y_hi: 4, y_lo: 2; y = y_hi * 2 + y_lo), z: 8, core: 2. Of those that a mesh axis runs over, the one named last changes fastest.
Arguments:
- queries: bfloat16 [16384, 64, 128], P(('dp', 'ctx'), 'tp'), parts along dimension 0, may hold values from -7 to 7, as said below
- keys: bfloat16 [16384, 8, 128], P(('dp', 'ctx'), 'tp'), parts along dimension 0, may hold values from -7 to 7, as said below
- values: bfloat16 [16384, 8, 128], P(('dp', 'ctx'), 'tp'), parts along dimension 0, may hold values from -6 to 6
- doc_lengths: int32 [48], P('dp'), parts along dimension 0, may hold values from 1 to 3072, 4096 in all
Outputs:
- attended: bfloat16 [16384, 64, 128], P(('dp', 'ctx'), 'tp'), parts along dimension 0
There are 4 independent parts, one for each index of `dp`. A program takes and returns all parts, laid end to end along the dimension named above; each array names one. Nothing has to cross between parts.
Inputs may be any that keep to these rules, and one draw needn't show every extreme that they name: `queries`: query entries lie within the bounds. `keys`: key entries lie within the bounds.
All inputs are finite; a program needn't handle non-finite values.
Results may differ from a plain program's by a relative error of at most 0.004.
Values may be sent and summed in bfloat16 or wider, within the bound.
No kernel may reach another device: no remote copies, remote signals or barrier semaphores. Data moves between devices by JAX's collectives and lax.ppermute only.
A program may use at most 64 MiB of HBM per device.

v0:
```python
import math

import jax
import jax.numpy as jnp
from jax import lax
from jax.sharding import PartitionSpec as P


def attention(query_block, query_pos, doc_starts, keys, values):
    row_count, head_count, head_size = query_block.shape
    kv_local = keys.shape[1]
    group_size = head_count // kv_local
    grouped_queries = query_block.reshape(row_count, kv_local, group_size, head_size)
    query_start = jnp.max(
        jnp.where(doc_starts[None, :] <= query_pos[:, None], doc_starts[None, :], 0), axis=1
    )
    score_scale = head_size ** (-0.5)
    start_state = (
        jnp.full((kv_local, group_size, row_count), -1e30, jnp.float32),
        jnp.zeros((kv_local, group_size, row_count), jnp.float32),
        jnp.zeros((kv_local, group_size, row_count, head_size), jnp.float32),
    )
    key_piece = lax.all_gather(keys, "ctx", axis=0, tiled=True)
    value_piece = lax.all_gather(values, "ctx", axis=0, tiled=True)
    key_count = key_piece.shape[0]
    tile_size = math.gcd(key_count, 512)

    def fold_tile(tile_index, tile_state):
        tile_offset = tile_index * tile_size
        key_block = lax.dynamic_slice_in_dim(key_piece, tile_offset, tile_size, 0)
        value_block = lax.dynamic_slice_in_dim(value_piece, tile_offset, tile_size, 0)
        key_pos = tile_offset + jnp.arange(tile_size, dtype=jnp.int32)
        row_best, row_total, weighted = tile_state
        tile_scores = (
            jnp.einsum(
                "rkgd,nkd->kgrn", grouped_queries, key_block, preferred_element_type=jnp.float32
            )
            * score_scale
        )
        visible_mask = (key_pos[None, :] <= query_pos[:, None]) & (
            key_pos[None, :] >= query_start[:, None]
        )
        tile_scores = jnp.where(visible_mask, tile_scores, -1e30)
        new_best = jnp.maximum(row_best, jnp.max(tile_scores, axis=-1))
        rescale = jnp.exp(row_best - new_best)
        tile_weights = jnp.where(visible_mask, jnp.exp(tile_scores - new_best[..., None]), 0.0)
        new_total = row_total * rescale + jnp.sum(tile_weights, axis=-1)
        new_weighted = weighted * rescale[..., None] + jnp.einsum(
            "kgrn,nkd->kgrd",
            tile_weights.astype(jnp.bfloat16),
            value_block,
            preferred_element_type=jnp.float32,
        )
        return (new_best, new_total, new_weighted)

    row_best, row_total, weighted = lax.fori_loop(0, key_count // tile_size, fold_tile, start_state)
    mixed = weighted / row_total[..., None]
    return (
        jnp.transpose(mixed, (2, 0, 1, 3))
        .reshape(row_count, head_count, head_size)
        .astype(jnp.bfloat16)
    )


def per_device(queries, keys, values, doc_lengths):
    row_count = queries.shape[0]
    my_index = lax.axis_index("ctx")
    doc_ends = jnp.cumsum(doc_lengths)
    doc_starts = doc_ends - doc_lengths
    row_ids = jnp.arange(row_count, dtype=jnp.int32)
    query_pos = my_index * row_count + row_ids
    return attention(queries, query_pos, doc_starts, keys, values)


def solution(mesh):
    placed = (
        P(("dp", "ctx"), "tp", None),
        P(("dp", "ctx"), "tp", None),
        P(("dp", "ctx"), "tp", None),
        P("dp"),
    )
    return jax.shard_map(
        per_device,
        mesh=mesh,
        in_specs=placed,
        out_specs=P(("dp", "ctx"), "tp", None),
        check_vma=False,
    )
```

profile of v0, /device:TPU:6, one launch (start us, length us, event | category | flops | bytes accessed | tf_op | source)
XLA Modules:
  0.0 170.3 jit_solution(3570628678628772545)
XLA Ops:
  6.5 0.7 all-gather.3.cloned.1.call-update
  7.3 0.7 all-gather.5.cloned.1.call-update
  8.0 0.8 reduce-window.9
  8.9 1.1 copy.20
  10.8 40.2 %all-gather.3.cloned.1.call-done = bf16[4096,1,128]{2,0,1:T(8,128)(2,1)} async-done(((bf16[256,1,128]{2,0,1:T(8,128)(2,1)}), bf16[4096,1,128]{2,0,1:T(8,128)(2,1)}) %all-gather.3.cloned.1.call-update) | async-done | bytes 1048592 | tf_op jit(solution)/shard_map/all_gather | solution.py:23
  51.0 40.0 %all-gather.5.cloned.1.call-done = bf16[4096,1,128]{2,0,1:T(8,128)(2,1)} async-done(((bf16[256,1,128]{2,0,1:T(8,128)(2,1)}), bf16[4096,1,128]{2,0,1:T(8,128)(2,1)}) %all-gather.5.cloned.1.call-update) | async-done | bytes 1048592 | tf_op jit(solution)/shard_map/all_gather | solution.py:24
  91.0 70.9 %while.18 = (s32[]{:T(128)}, f32[1,8,256]{2,1,0:T(8,128)S(1)}, f32[1,8,256]{2,1,0:T(8,128)S(1)}, f32[1,8,256,128]{3,2,1,0:T(8,128)S(1)}, s32[256]{0:T(256)S(1)},...) while((s32[]{:T(128)}, f32[1,8,256]{2,1,0:T(8,128)S(1)}, ...), condition=%wide.region_5.6_spmd.clone, body=%wide.region_2.5_spmd.clone.sunk | while | flops 551695104 | bytes 32906464 | solution.py:56
  91.1 3.6 %fusion.37 = (f32[8,256]{1,0:T(8,128)S(1)}, f32[512,256,8]{1,0,2:T(8,128)}) fusion(pred[256,512]{0,1:T(8,128)(4,1)S(1)} %compare_and_fusion.2, bf16[256,1,8,128]{3,0,2,1:T(8,128)(2,1)S(1)} %get-tuple-element.312, bf16[4096,1,128]{2,0,1:T(8,128)(2,1)} %get-tuple-element.311, s32[]{:T(128)S(6)} %select_n.71), kind=kOutput, calls=%fused_computation.3.clone.1 | convolution fusion | flops 271579136 | bytes 4988932 | tf_op jit(solution)/shard_map/while/body/eval_jaxpr/rkgd,nkd->kgrn/dot_general | solution.py:35
  94.8 4.0 %fusion.40 = f32[1,8,256,128]{3,2,1,0:T(8,128)S(1)} fusion(f32[512,256,8]{1,0,2:T(8,128)} %get-tuple-element.278, f32[8,256]{1,0:T(8,128)S(1)} %bitcast.87, pred[256,512]{0,1:T(8,128)(4,1)S(1)} %compare_and_fusion.2, f32[1,8,256,128]{3,2,1,0:T(8,128)S(1)} %get-tuple-element.296, f32[8,256]{1,0:T(8,128)S(1)} %get-tuple-element.279, pred[]{:T(512)S(6)} %compare.3, ...), kind=kOutput, calls=%fused_computation.10.clone.1 | convolution fusion | flops 274464768 | bytes 6569989 | tf_op jit(solution)/shard_map/while/body/eval_jaxpr/kgrn,nkd->kgrd/dot_general | solution.py:48
  98.7 1.0 fusion.39
  100.0 3.6 %fusion.37 = (f32[8,256]{1,0:T(8,128)S(1)}, f32[512,256,8]{1,0,2:T(8,128)}) fusion(pred[256,512]{0,1:T(8,128)(4,1)S(1)} %compare_and_fusion.2, bf16[256,1,8,128]{3,0,2,1:T(8,128)(2,1)S(1)} %get-tuple-element.312, bf16[4096,1,128]{2,0,1:T(8,128)(2,1)} %get-tuple-element.311, s32[]{:T(128)S(6)} %select_n.71), kind=kOutput, calls=%fused_computation.3.clone.1 | convolution fusion | flops 271579136 | bytes 4988932 | tf_op jit(solution)/shard_map/while/body/eval_jaxpr/rkgd,nkd->kgrn/dot_general | solution.py:35
  103.6 4.0 %fusion.40 = f32[1,8,256,128]{3,2,1,0:T(8,128)S(1)} fusion(f32[512,256,8]{1,0,2:T(8,128)} %get-tuple-element.278, f32[8,256]{1,0:T(8,128)S(1)} %bitcast.87, pred[256,512]{0,1:T(8,128)(4,1)S(1)} %compare_and_fusion.2, f32[1,8,256,128]{3,2,1,0:T(8,128)S(1)} %get-tuple-element.296, f32[8,256]{1,0:T(8,128)S(1)} %get-tuple-element.279, pred[]{:T(512)S(6)} %compare.3, ...), kind=kOutput, calls=%fused_computation.10.clone.1 | convolution fusion | flops 274464768 | bytes 6569989 | tf_op jit(solution)/shard_map/while/body/eval_jaxpr/kgrn,nkd->kgrd/dot_general | solution.py:48
  107.6 1.0 fusion.39
  108.9 3.6 %fusion.37 = (f32[8,256]{1,0:T(8,128)S(1)}, f32[512,256,8]{1,0,2:T(8,128)}) fusion(pred[256,512]{0,1:T(8,128)(4,1)S(1)} %compare_and_fusion.2, bf16[256,1,8,128]{3,0,2,1:T(8,128)(2,1)S(1)} %get-tuple-element.312, bf16[4096,1,128]{2,0,1:T(8,128)(2,1)} %get-tuple-element.311, s32[]{:T(128)S(6)} %select_n.71), kind=kOutput, calls=%fused_computation.3.clone.1 | convolution fusion | flops 271579136 | bytes 4988932 | tf_op jit(solution)/shard_map/while/body/eval_jaxpr/rkgd,nkd->kgrn/dot_general | solution.py:35
  112.5 4.0 %fusion.40 = f32[1,8,256,128]{3,2,1,0:T(8,128)S(1)} fusion(f32[512,256,8]{1,0,2:T(8,128)} %get-tuple-element.278, f32[8,256]{1,0:T(8,128)S(1)} %bitcast.87, pred[256,512]{0,1:T(8,128)(4,1)S(1)} %compare_and_fusion.2, f32[1,8,256,128]{3,2,1,0:T(8,128)S(1)} %get-tuple-element.296, f32[8,256]{1,0:T(8,128)S(1)} %get-tuple-element.279, pred[]{:T(512)S(6)} %compare.3, ...), kind=kOutput, calls=%fused_computation.10.clone.1 | convolution fusion | flops 274464768 | bytes 6569989 | tf_op jit(solution)/shard_map/while/body/eval_jaxpr/kgrn,nkd->kgrd/dot_general | solution.py:48
  116.5 1.0 fusion.39
  117.7 3.6 %fusion.37 = (f32[8,256]{1,0:T(8,128)S(1)}, f32[512,256,8]{1,0,2:T(8,128)}) fusion(pred[256,512]{0,1:T(8,128)(4,1)S(1)} %compare_and_fusion.2, bf16[256,1,8,128]{3,0,2,1:T(8,128)(2,1)S(1)} %get-tuple-element.312, bf16[4096,1,128]{2,0,1:T(8,128)(2,1)} %get-tuple-element.311, s32[]{:T(128)S(6)} %select_n.71), kind=kOutput, calls=%fused_computation.3.clone.1 | convolution fusion | flops 271579136 | bytes 4988932 | tf_op jit(solution)/shard_map/while/body/eval_jaxpr/rkgd,nkd->kgrn/dot_general | solution.py:35
  121.4 4.0 %fusion.40 = f32[1,8,256,128]{3,2,1,0:T(8,128)S(1)} fusion(f32[512,256,8]{1,0,2:T(8,128)} %get-tuple-element.278, f32[8,256]{1,0:T(8,128)S(1)} %bitcast.87, pred[256,512]{0,1:T(8,128)(4,1)S(1)} %compare_and_fusion.2, f32[1,8,256,128]{3,2,1,0:T(8,128)S(1)} %get-tuple-element.296, f32[8,256]{1,0:T(8,128)S(1)} %get-tuple-element.279, pred[]{:T(512)S(6)} %compare.3, ...), kind=kOutput, calls=%fused_computation.10.clone.1 | convolution fusion | flops 274464768 | bytes 6569989 | tf_op jit(solution)/shard_map/while/body/eval_jaxpr/kgrn,nkd->kgrd/dot_general | solution.py:48
  125.3 1.0 fusion.39
  126.6 3.6 %fusion.37 = (f32[8,256]{1,0:T(8,128)S(1)}, f32[512,256,8]{1,0,2:T(8,128)}) fusion(pred[256,512]{0,1:T(8,128)(4,1)S(1)} %compare_and_fusion.2, bf16[256,1,8,128]{3,0,2,1:T(8,128)(2,1)S(1)} %get-tuple-element.312, bf16[4096,1,128]{2,0,1:T(8,128)(2,1)} %get-tuple-element.311, s32[]{:T(128)S(6)} %select_n.71), kind=kOutput, calls=%fused_computation.3.clone.1 | convolution fusion | flops 271579136 | bytes 4988932 | tf_op jit(solution)/shard_map/while/body/eval_jaxpr/rkgd,nkd->kgrn/dot_general | solution.py:35
  130.2 4.0 %fusion.40 = f32[1,8,256,128]{3,2,1,0:T(8,128)S(1)} fusion(f32[512,256,8]{1,0,2:T(8,128)} %get-tuple-element.278, f32[8,256]{1,0:T(8,128)S(1)} %bitcast.87, pred[256,512]{0,1:T(8,128)(4,1)S(1)} %compare_and_fusion.2, f32[1,8,256,128]{3,2,1,0:T(8,128)S(1)} %get-tuple-element.296, f32[8,256]{1,0:T(8,128)S(1)} %get-tuple-element.279, pred[]{:T(512)S(6)} %compare.3, ...), kind=kOutput, calls=%fused_computation.10.clone.1 | convolution fusion | flops 274464768 | bytes 6569989 | tf_op jit(solution)/shard_map/while/body/eval_jaxpr/kgrn,nkd->kgrd/dot_general | solution.py:48
  134.2 1.0 fusion.39
  135.5 3.6 %fusion.37 = (f32[8,256]{1,0:T(8,128)S(1)}, f32[512,256,8]{1,0,2:T(8,128)}) fusion(pred[256,512]{0,1:T(8,128)(4,1)S(1)} %compare_and_fusion.2, bf16[256,1,8,128]{3,0,2,1:T(8,128)(2,1)S(1)} %get-tuple-element.312, bf16[4096,1,128]{2,0,1:T(8,128)(2,1)} %get-tuple-element.311, s32[]{:T(128)S(6)} %select_n.71), kind=kOutput, calls=%fused_computation.3.clone.1 | convolution fusion | flops 271579136 | bytes 4988932 | tf_op jit(solution)/shard_map/while/body/eval_jaxpr/rkgd,nkd->kgrn/dot_general | solution.py:35
  139.1 4.0 %fusion.40 = f32[1,8,256,128]{3,2,1,0:T(8,128)S(1)} fusion(f32[512,256,8]{1,0,2:T(8,128)} %get-tuple-element.278, f32[8,256]{1,0:T(8,128)S(1)} %bitcast.87, pred[256,512]{0,1:T(8,128)(4,1)S(1)} %compare_and_fusion.2, f32[1,8,256,128]{3,2,1,0:T(8,128)S(1)} %get-tuple-element.296, f32[8,256]{1,0:T(8,128)S(1)} %get-tuple-element.279, pred[]{:T(512)S(6)} %compare.3, ...), kind=kOutput, calls=%fused_computation.10.clone.1 | convolution fusion | flops 274464768 | bytes 6569989 | tf_op jit(solution)/shard_map/while/body/eval_jaxpr/kgrn,nkd->kgrd/dot_general | solution.py:48
  143.1 1.0 fusion.39
  144.3 3.6 %fusion.37 = (f32[8,256]{1,0:T(8,128)S(1)}, f32[512,256,8]{1,0,2:T(8,128)}) fusion(pred[256,512]{0,1:T(8,128)(4,1)S(1)} %compare_and_fusion.2, bf16[256,1,8,128]{3,0,2,1:T(8,128)(2,1)S(1)} %get-tuple-element.312, bf16[4096,1,128]{2,0,1:T(8,128)(2,1)} %get-tuple-element.311, s32[]{:T(128)S(6)} %select_n.71), kind=kOutput, calls=%fused_computation.3.clone.1 | convolution fusion | flops 271579136 | bytes 4988932 | tf_op jit(solution)/shard_map/while/body/eval_jaxpr/rkgd,nkd->kgrn/dot_general | solution.py:35
  147.9 4.0 %fusion.40 = f32[1,8,256,128]{3,2,1,0:T(8,128)S(1)} fusion(f32[512,256,8]{1,0,2:T(8,128)} %get-tuple-element.278, f32[8,256]{1,0:T(8,128)S(1)} %bitcast.87, pred[256,512]{0,1:T(8,128)(4,1)S(1)} %compare_and_fusion.2, f32[1,8,256,128]{3,2,1,0:T(8,128)S(1)} %get-tuple-element.296, f32[8,256]{1,0:T(8,128)S(1)} %get-tuple-element.279, pred[]{:T(512)S(6)} %compare.3, ...), kind=kOutput, calls=%fused_computation.10.clone.1 | convolution fusion | flops 274464768 | bytes 6569989 | tf_op jit(solution)/shard_map/while/body/eval_jaxpr/kgrn,nkd->kgrd/dot_general | solution.py:48
  151.9 1.0 fusion.39
  153.2 3.6 %fusion.37 = (f32[8,256]{1,0:T(8,128)S(1)}, f32[512,256,8]{1,0,2:T(8,128)}) fusion(pred[256,512]{0,1:T(8,128)(4,1)S(1)} %compare_and_fusion.2, bf16[256,1,8,128]{3,0,2,1:T(8,128)(2,1)S(1)} %get-tuple-element.312, bf16[4096,1,128]{2,0,1:T(8,128)(2,1)} %get-tuple-element.311, s32[]{:T(128)S(6)} %select_n.71), kind=kOutput, calls=%fused_computation.3.clone.1 | convolution fusion | flops 271579136 | bytes 4988932 | tf_op jit(solution)/shard_map/while/body/eval_jaxpr/rkgd,nkd->kgrn/dot_general | solution.py:35
  156.8 4.0 %fusion.40 = f32[1,8,256,128]{3,2,1,0:T(8,128)S(1)} fusion(f32[512,256,8]{1,0,2:T(8,128)} %get-tuple-element.278, f32[8,256]{1,0:T(8,128)S(1)} %bitcast.87, pred[256,512]{0,1:T(8,128)(4,1)S(1)} %compare_and_fusion.2, f32[1,8,256,128]{3,2,1,0:T(8,128)S(1)} %get-tuple-element.296, f32[8,256]{1,0:T(8,128)S(1)} %get-tuple-element.279, pred[]{:T(512)S(6)} %compare.3, ...), kind=kOutput, calls=%fused_computation.10.clone.1 | convolution fusion | flops 274464768 | bytes 6569989 | tf_op jit(solution)/shard_map/while/body/eval_jaxpr/kgrn,nkd->kgrd/dot_general | solution.py:48
  160.8 1.0 fusion.39
  162.0 1.5 fusion.28
  (73 shorter events, 2.6 us)
Async XLA Ops:
  6.5 44.4 %all-gather.3.cloned.1.call-start = ((), (), s32[]{:S(2)}) async-start(), calls=%async_computation | async-start | bytes 1114112 | tf_op jit(solution)/shard_map/all_gather | solution.py:23
  7.3 83.7 %all-gather.5.cloned.1.call-start = ((), (), s32[]{:S(2)}) async-start(), calls=%async_computation.1 | async-start | bytes 1114112 | tf_op jit(solution)/shard_map/all_gather | solution.py:24
  94.8 4.0 %copy-start = (f32[512,256,8]{1,0,2:T(8,128)S(1)}, f32[512,256,8]{1,0,2:T(8,128)}, u32[]{:S(2)}) copy-start(f32[512,256,8]{1,0,2:T(8,128)} %get-tuple-element.278) | copy-start | bytes 12582916 | tf_op jit(solution)/shard_map/while
  103.6 4.0 %copy-start = (f32[512,256,8]{1,0,2:T(8,128)S(1)}, f32[512,256,8]{1,0,2:T(8,128)}, u32[]{:S(2)}) copy-start(f32[512,256,8]{1,0,2:T(8,128)} %get-tuple-element.278) | copy-start | bytes 12582916 | tf_op jit(solution)/shard_map/while
  112.5 4.0 %copy-start = (f32[512,256,8]{1,0,2:T(8,128)S(1)}, f32[512,256,8]{1,0,2:T(8,128)}, u32[]{:S(2)}) copy-start(f32[512,256,8]{1,0,2:T(8,128)} %get-tuple-element.278) | copy-start | bytes 12582916 | tf_op jit(solution)/shard_map/while
  121.4 4.0 %copy-start = (f32[512,256,8]{1,0,2:T(8,128)S(1)}, f32[512,256,8]{1,0,2:T(8,128)}, u32[]{:S(2)}) copy-start(f32[512,256,8]{1,0,2:T(8,128)} %get-tuple-element.278) | copy-start | bytes 12582916 | tf_op jit(solution)/shard_map/while
  130.2 4.0 %copy-start = (f32[512,256,8]{1,0,2:T(8,128)S(1)}, f32[512,256,8]{1,0,2:T(8,128)}, u32[]{:S(2)}) copy-start(f32[512,256,8]{1,0,2:T(8,128)} %get-tuple-element.278) | copy-start | bytes 12582916 | tf_op jit(solution)/shard_map/while
  139.1 4.0 %copy-start = (f32[512,256,8]{1,0,2:T(8,128)S(1)}, f32[512,256,8]{1,0,2:T(8,128)}, u32[]{:S(2)}) copy-start(f32[512,256,8]{1,0,2:T(8,128)} %get-tuple-element.278) | copy-start | bytes 12582916 | tf_op jit(solution)/shard_map/while
  147.9 4.0 %copy-start = (f32[512,256,8]{1,0,2:T(8,128)S(1)}, f32[512,256,8]{1,0,2:T(8,128)}, u32[]{:S(2)}) copy-start(f32[512,256,8]{1,0,2:T(8,128)} %get-tuple-element.278) | copy-start | bytes 12582916 | tf_op jit(solution)/shard_map/while
  156.8 4.0 %copy-start = (f32[512,256,8]{1,0,2:T(8,128)S(1)}, f32[512,256,8]{1,0,2:T(8,128)}, u32[]{:S(2)}) copy-start(f32[512,256,8]{1,0,2:T(8,128)} %get-tuple-element.278) | copy-start | bytes 12582916 | tf_op jit(solution)/shard_map/while
Sparse Core Ops, SparseCore 0:
  9.5 41.4 all-gather.2
  53.1 37.8 all-gather.4
where the time goes:
time: 173 us; the launch traced here: 170 us
  waiting for transfers between devices  81.6 us (47%)
  matrix products  60.5 us (35%)
  between operations  13.5 us (8%)
  other arithmetic  12.8 us (7%)
    all_gather x1, waiting for transfers between devices, attention(): key_piece = lax.all_gather(keys, 'ctx', axis=0, tiled=True)  40.2 us
    all_gather x1, waiting for transfers between devices, attention(): value_piece = lax.all_gather(values, 'ctx', axis=0, tiled=True)  40 us
    dot_general x8, matrix products, fold_tile(): jnp.einsum('kgrn,nkd->kgrd', tile_weights.astype(jnp.bfloat16), value_blo...  31.7 us
    dot_general x8, matrix products, fold_tile(): jnp.einsum('rkgd,nkd->kgrn', grouped_queries, key_block, preferred_elemen...  28.8 us
    reduce_sum x8, other arithmetic, fold_tile(): new_total = row_total * rescale + jnp.sum(tile_weights, axis=-1)  8.08 us
  transfers between devices with their start and end apart: 2, of which 2 were waited for; matrix products, arithmetic and copies ran while one was open for 2% of the time, Pallas kernels for 0%

commit v1 on v0

v1 whole, which is shorter than its diff:
```python
import functools

import jax
import jax.numpy as jnp
from jax import lax
from jax.experimental import pallas as pl
from jax.experimental.pallas import tpu as pltpu
from jax.sharding import PartitionSpec as P

HEAD = 128
CHUNK = 256
LOG2_SCALE = HEAD**-0.5 * 1.4426950408889634
LOWEST = -1e30


def flash(lengths, q, mine, theirs, out, best, total, acc, starts):
    rows = q.shape[0]
    group = rows // CHUNK
    position = lax.axis_index("ctx")
    core = lax.rem(position, 2)
    tile_id = position // 2
    first = position * CHUNK
    last = first + CHUNK - 1
    token = first + lax.broadcasted_iota(jnp.int32, (CHUNK, HEAD), 0)
    begin = jnp.int32(0)
    first_start, last_start = jnp.int32(0), jnp.int32(0)
    token_start = jnp.zeros((CHUNK, HEAD), jnp.int32)
    for doc in range(lengths.shape[0]):
        token_start = jnp.where(token >= begin, begin, token_start)
        first_start = jnp.where(first >= begin, begin, first_start)
        last_start = jnp.where(last >= begin, begin, last_start)
        begin = begin + lengths[doc]
    for head in range(group):
        starts[pl.ds(head, CHUNK, stride=group), :] = token_start
    best[...] = jnp.full(best.shape, LOWEST, jnp.float32)
    total[...] = jnp.zeros(total.shape, jnp.float32)
    acc[...] = jnp.zeros(acc.shape, jnp.float32)

    def fold(tile, masked):
        halves = ((mine, 2 * tile + core), (theirs, 2 * tile + 1 - core))
        scores = [
            lax.dot_general(
                q[...], ref[tile, 0], (((1,), (1,)), ((), ())), preferred_element_type=jnp.float32
            )
            for ref, _ in halves
        ]
        blocks = []
        for part, (_, chunk) in zip(scores, halves):
            for j in range(0, CHUNK, HEAD):
                block = part[:, j : j + HEAD]
                if masked:
                    key = chunk * CHUNK + j + lax.broadcasted_iota(jnp.int32, block.shape, 1)
                    row = first + lax.broadcasted_iota(jnp.int32, block.shape, 0) // group
                    block = jnp.where((key >= starts[...]) & (key <= row), block, LOWEST)
                blocks.append(block)
        peak = functools.reduce(jnp.maximum, blocks)
        old = best[...]
        new = jnp.maximum(old, jnp.max(peak, axis=1, keepdims=True))
        shrink = jnp.exp2((old - new) * LOG2_SCALE)
        base = new * LOG2_SCALE
        weights = [jnp.exp2(block * LOG2_SCALE - base) for block in blocks]
        best[...] = new
        total[...] = total[...] * shrink + sum(weights)
        low = [w.astype(jnp.bfloat16) for w in weights]
        half = len(low) // 2
        added = jnp.dot(
            jnp.concatenate(low[:half], 1), mine[tile, 1], preferred_element_type=jnp.float32
        ) + jnp.dot(
            jnp.concatenate(low[half:], 1), theirs[tile, 1], preferred_element_type=jnp.float32
        )
        acc[...] = acc[...] * shrink + added

    fold(tile_id, True)

    def step(tile, carry):
        clear = tile * 2 * CHUNK >= last_start

        @pl.when(clear)
        def _():
            fold(tile, False)

        @pl.when(jnp.logical_not(clear))
        def _():
            fold(tile, True)

        return carry

    lax.fori_loop(first_start // (2 * CHUNK), tile_id, step, 0)
    out[...] = (acc[...] / jnp.sum(total[...], axis=1, keepdims=True)).astype(out.dtype)


def per_device(queries, keys, values, doc_lengths):
    tokens, heads, _ = queries.shape
    rows = tokens * heads
    q = queries.reshape(rows, HEAD)
    kv = jnp.stack([keys[:, 0], values[:, 0]])
    spread = jnp.broadcast_to(kv[None], (8,) + kv.shape)
    groups = [[2 * i + core for i in range(8)] for core in range(2)]
    mine = lax.all_to_all(spread, "ctx", 0, 0, axis_index_groups=groups)
    theirs = lax.ppermute(mine, "ctx", [(i, i ^ 1) for i in range(16)])
    vmem = pl.BlockSpec(memory_space=pltpu.VMEM)
    out = pl.pallas_call(
        flash,
        out_shape=jax.ShapeDtypeStruct((rows, HEAD), jnp.bfloat16),
        in_specs=[pl.BlockSpec(memory_space=pltpu.SMEM), vmem, vmem, vmem],
        out_specs=vmem,
        scratch_shapes=[pltpu.VMEM((rows, HEAD), jnp.float32)] * 3
        + [pltpu.VMEM((rows, HEAD), jnp.int32)],
        compiler_params=pltpu.CompilerParams(vmem_limit_bytes=48 * 2**20),
    )(doc_lengths, q, mine, theirs)
    return out.reshape(queries.shape)


def solution(mesh):
    placed = (
        P(("dp", "ctx"), "tp", None),
        P(("dp", "ctx"), "tp", None),
        P(("dp", "ctx"), "tp", None),
        P("dp"),
    )
    return jax.shard_map(
        per_device,
        mesh=mesh,
        in_specs=placed,
        out_specs=P(("dp", "ctx"), "tp", None),
        check_vma=False,
    )
```

time: 173 us -> 42 us (0.24)
  the two profiles are of different devices: /device:TPU:6 before, /device:TPU:415 now
where the time goes in v1:
time: 42 us; the launch traced here: 41.8 us
  blocking collectives  17.6 us (42%)
  Pallas kernels  17 us (40%)
  starting transfers between devices  3.85 us (9%)
  waiting for transfers between devices  2.26 us (5%)
  other arithmetic  0.88 us (2%)
    all_to_all x1, blocking collectives, per_device(): mine = lax.all_to_all(spread, 'ctx', 0, 0, axis_index_groups=groups)  17.6 us
    pallas_call x1, Pallas kernels, per_device(): pl.pallas_call(flash, out_shape=jax.ShapeDtypeStruct((rows, HEAD), jnp.bf...  17 us
    ppermute x1, starting transfers between devices, per_device(): theirs = lax.ppermute(mine, 'ctx', [(i, i ^ 1) for i in range(16)])  3.85 us
    ppermute x1, waiting for transfers between devices, per_device(): theirs = lax.ppermute(mine, 'ctx', [(i, i ^ 1) for i in range(16)])  2.26 us
    another operation x1, other arithmetic, per_device(): kv = jnp.stack([keys[:, 0], values[:, 0]])  0.88 us
  transfers between devices with their start and end apart: 1, of which 1 were waited for; matrix products, arithmetic and copies ran while one was open for 0% of the time, Pallas kernels for 0%

profile of v1, /device:TPU:415, one launch (start us, length us, event | category | flops | bytes accessed | tf_op | source)
XLA Modules:
  0.0 41.8 jit_solution(17330805303688550110)
XLA Ops:
  0.0 0.9 %pad_maximum_fusion = bf16[2,256,128]{2,1,0:T(8,128)(2,1)S(1)} fusion(bf16[1,256,128]{2,1,0:T(8,128)(2,1)} %bitcast.5, bf16[1,256,128]{2,1,0:T(8,128)(2,1)} %bitcast.6), kind=kLoop, calls=%fused_computation | loop fusion | flops 65536 | bytes 262144 | tf_op jit(solution)/shard_map/stack | solution.py:96
  0.9 0.2 broadcast_in_dim.2
  1.1 0.0 copy-start
  1.1 17.6 %all_to_all.5.mine = bf16[8,2,256,128]{3,2,1,0:T(8,128)(2,1)S(1)} all-to-all(bf16[8,2,256,128]{3,2,1,0:T(8,128)(2,1)S(1)} %broadcast_in_dim.2), channel_id=1, replica_groups={{0,16,32,48,64,80,96,112},{8,24,40,56,72,88,104,120},{1,17,33,49,65,81,..., dimensions={0} | all-to-all | bytes 2097152 | tf_op jit(solution)/shard_map/all_to_all | solution.py:99
  18.7 0.0 copy-start.1
  18.7 3.8 %collective-permute-start = (bf16[8,2,256,128]{3,2,1,0:T(8,128)(2,1)S(1)}, bf16[8,2,256,128]{3,2,1,0:T(8,128)(2,1)S(1)}, u32[]{:S(2)}, u32[]{:S(2)}) collective-permute-start(bf16[8,2,256,128]{3,2,1,0:T(8,128)(2,1)S(1)} %all_to_all.5.mine), channel_id=1, source_target_pairs={{0,8},{8,0},{16,24},{24,16},{32,40},{40,32},{48,56},{56,48},{64,72... | collective-permute-start | bytes 3145736 | tf_op jit(solution)/shard_map/ppermute | solution.py:100
  22.6 2.3 %collective-permute-done.theirs = bf16[8,2,256,128]{3,2,1,0:T(8,128)(2,1)S(1)} collective-permute-done((bf16[8,2,256,128]{3,2,1,0:T(8,128)(2,1)S(1)}, bf16[8,2,256,128]{3,2,1,0:T(8,128)(2,1)S(1)}, u32[]{:S(2)}, u32[]{:S(2)}) %collective-permute-start) | collective-permute-done | bytes 1048608 | tf_op jit(solution)/shard_map/ppermute | solution.py:100
  24.8 0.0 copy-done
  24.8 0.0 copy-done.1
  24.8 17.0 %shard_map.46 = bf16[2048,128]{1,0:T(8,128)(2,1)} custom-call(s32[12]{0:T(128)S(1)} %copy-done.1, bf16[2048,128]{1,0:T(8,128)(2,1)S(1)} %bitcast.4, bf16[8,2,256,128]{3,2,1,0:T(8,128)(2,1)S(1)} %all_to_all.5.mine, bf16[8,2,256,128]{3,2,1,0:T(8,128)(2,1)S(1)} %collective-permute-done.theirs), custom_call_target="tpu_custom_call" | custom-call | tf_op jit(solution)/shard_map/pallas_call | solution.py:102
Async XLA Ops:
  1.1 23.7 %copy-start = (bf16[256,8,128]{2,1,0:T(8,128)(2,1)S(1)}, bf16[256,8,128]{2,1,0:T(8,128)(2,1)}, u32[]{:S(2)}) copy-start(bf16[256,8,128]{2,1,0:T(8,128)(2,1)} %param.4) | copy-start | bytes 1572868
  18.7 6.1 %copy-start.1 = (s32[12]{0:T(128)S(1)}, s32[12]{0:T(128)}, u32[]{:S(2)}) copy-start(s32[12]{0:T(128)} %lengths.1) | copy-start | bytes 148
  18.7 6.1 %collective-permute-start = (bf16[8,2,256,128]{3,2,1,0:T(8,128)(2,1)S(1)}, bf16[8,2,256,128]{3,2,1,0:T(8,128)(2,1)S(1)}, u32[]{:S(2)}, u32[]{:S(2)}) collective-permute-start(bf16[8,2,256,128]{3,2,1,0:T(8,128)(2,1)S(1)} %all_to_all.5.mine), channel_id=1, source_target_pairs={{0,8},{8,0},{16,24},{24,16},{32,40},{40,32},{48,56},{56,48},{64,72... | collective-permute-start | bytes 3145736 | tf_op jit(solution)/shard_map/ppermute | solution.py:100

commit v2 on v1

v2 whole, which is shorter than its diff:
```python
import functools

import jax
import jax.numpy as jnp
from jax import lax
from jax.experimental import pallas as pl
from jax.experimental.pallas import tpu as pltpu
from jax.sharding import PartitionSpec as P

HEAD = 128
CHUNK = 256
BLOCK = 512
LOG2_SCALE = HEAD**-0.5 * 1.4426950408889634
LOWEST = -1e30
HIDDEN = 1e30
SLACK = 40.0 / LOG2_SCALE
VMEM_LIMIT = 20 * 2**20


def place(lengths):
    position = lax.axis_index("ctx")
    first = position * CHUNK
    begin = jnp.int32(0)
    first_start = jnp.int32(0)
    begins = []
    for doc in range(lengths.shape[0]):
        begins.append(begin)
        first_start = jnp.where(first >= begin, begin, first_start)
        begin = begin + lengths[doc]
    return position, first, first_start, begins


def scores(q, key):
    return lax.dot_general(q, key, (((1,), (1,)), ((), ())), preferred_element_type=jnp.float32)


def split(block):
    return [block[:, j : j + HEAD] for j in range(0, CHUNK, HEAD)]


def hide(block, chunk, first, row0, group, starts):
    done = []
    for j, part in enumerate(split(block)):
        key = chunk * CHUNK + j * HEAD + lax.broadcasted_iota(jnp.int32, part.shape, 1)
        row = first + (row0 + lax.broadcasted_iota(jnp.int32, part.shape, 0)) // group
        done.append(jnp.where((key >= starts) & (key <= row), part, LOWEST))
    return jnp.concatenate(done, 1)


def local_kernel(lengths, q, own, partner, best, total, acc, starts):
    rows = q.shape[0]
    group = rows // CHUNK
    position, first, first_start, begins = place(lengths)
    core = lax.rem(position, 2)
    token = first + lax.broadcasted_iota(jnp.int32, (CHUNK, HEAD), 0)
    token_start = jnp.zeros((CHUNK, HEAD), jnp.int32)
    for begin in begins:
        token_start = jnp.where(token >= begin, begin, token_start)
    for head in range(group):
        starts[pl.ds(head, CHUNK, stride=group), :] = token_start
    best[...] = jnp.full(best.shape, LOWEST, jnp.float32)
    total[...] = jnp.zeros(total.shape, jnp.float32)
    acc[...] = jnp.zeros(acc.shape, jnp.float32)

    def fold(ref, chunk):
        def block(i, carry):
            rs = pl.ds(pl.multiple_of(i * BLOCK, BLOCK), BLOCK)
            s = hide(scores(q[rs, :], ref[0]), chunk, first, i * BLOCK, group, starts[rs, :])
            old = best[rs, :]
            new = jnp.maximum(old, jnp.max(s, axis=1, keepdims=True))
            shrink = jnp.exp2((old - new) * LOG2_SCALE)
            base = new * LOG2_SCALE
            weights = [jnp.exp2(part * LOG2_SCALE - base) for part in split(s)]
            best[rs, :] = new
            total[rs, :] = total[rs, :] * shrink + sum(weights)
            low = jnp.concatenate([w.astype(jnp.bfloat16) for w in weights], 1)
            acc[rs, :] = acc[rs, :] * shrink + jnp.dot(
                low, ref[1], preferred_element_type=jnp.float32
            )
            return carry

        lax.fori_loop(0, rows // BLOCK, block, 0)

    @pl.when(core == 1)
    def _():
        fold(partner, position - 1)

    fold(own, position)
    best[...] = jnp.where(starts[...] == first_start, best[...], HIDDEN)


def fold_chunks(lengths, q, kv, best, total, acc, here, there, mine):
    rows = q.shape[0]
    position, _, first_start, _ = place(lengths)
    core = lax.rem(position, 2)
    core = core if mine else 1 - core
    lo = (first_start // CHUNK - core + 1) // 2
    hi = position // 2

    def excess_of(s, rs):
        excess = functools.reduce(jnp.maximum, split(s)) - best[rs, :]
        return jnp.max(excess.reshape(BLOCK // 8, 8, HEAD), axis=0)

    def flag_of(over):
        return (jnp.max(over) > SLACK).astype(jnp.int32)

    def first_scores():
        key = (2 * lo + core) * CHUNK + lax.broadcasted_iota(jnp.int32, (1, CHUNK), 1)
        seen = key >= first_start
        over = None
        for r in range(0, rows, BLOCK):
            rs = slice(r, r + BLOCK)
            s = jnp.where(seen, scores(q[rs, :], kv[lo, 0]), LOWEST)
            here[rs, :] = s
            excess = excess_of(s, rs)
            over = excess if over is None else jnp.maximum(over, excess)
        return flag_of(over)

    def mend(now):
        def block(i, carry):
            rs = pl.ds(pl.multiple_of(i * BLOCK, BLOCK), BLOCK)
            old = best[rs, :]
            new = jnp.maximum(old, jnp.max(now[rs, :], axis=1, keepdims=True))
            shrink = jnp.exp2((old - new) * LOG2_SCALE)
            best[rs, :] = new
            total[rs, :] = total[rs, :] * shrink
            acc[rs, :] = acc[rs, :] * shrink
            return carry

        lax.fori_loop(0, rows // BLOCK, block, 0)

    def step(tile, now, later, stale):
        @pl.when(stale > 0)
        def _():
            mend(now)

        ahead = jnp.minimum(tile + 1, hi - 1)
        over = None
        for r in range(0, rows, BLOCK):
            rs = slice(r, r + BLOCK)
            s = scores(q[rs, :], kv[ahead, 0])
            later[rs, :] = s
            excess = excess_of(s, rs)
            over = excess if over is None else jnp.maximum(over, excess)
            base = best[rs, :] * LOG2_SCALE
            weights = [jnp.exp2(part * LOG2_SCALE - base) for part in split(now[rs, :])]
            total[rs, :] += sum(weights)
            low = jnp.concatenate([w.astype(jnp.bfloat16) for w in weights], 1)
            acc[rs, :] += jnp.dot(low, kv[tile, 1], preferred_element_type=jnp.float32)
        return flag_of(over)

    @pl.when(lo < hi)
    def _():
        stale = first_scores()

        def pair(i, stale):
            tile = lo + 2 * i
            stale = step(tile, here, there, stale)
            return lax.cond(
                tile + 1 < hi,
                lambda flag: step(tile + 1, there, here, flag),
                lambda flag: flag,
                stale,
            )

        lax.fori_loop(0, (hi - lo + 1) // 2, pair, stale)


def middle_kernel(
    lengths, q, kv, best_in, total_in, acc_in, best, total, acc, here, there
):
    best[...], total[...], acc[...] = best_in[...], total_in[...], acc_in[...]
    fold_chunks(lengths, q, kv, best, total, acc, here, there, True)


def last_kernel(
    lengths, q, kv, best_in, total_in, acc_in, out, best, total, acc, here, there
):
    best[...], total[...], acc[...] = best_in[...], total_in[...], acc_in[...]
    fold_chunks(lengths, q, kv, best, total, acc, here, there, False)
    for r in range(0, out.shape[0], BLOCK):
        rs = slice(r, r + BLOCK)
        out[rs, :] = (acc[rs, :] / jnp.sum(total[rs, :], axis=1, keepdims=True)).astype(out.dtype)


def per_device(queries, keys, values, doc_lengths):
    tokens, heads, _ = queries.shape
    rows = tokens * heads
    q = queries.reshape(rows, HEAD)
    spread = jnp.broadcast_to(
        jnp.stack([keys[:, 0], values[:, 0]])[None], (8, 2, tokens, HEAD)
    )
    near_keys, near_values = lax.optimization_barrier((keys, values))
    kv = jnp.stack([near_keys[:, 0], near_values[:, 0]])
    groups = [[2 * i + core for i in range(8)] for core in range(2)]
    swap = [(i, i ^ 1) for i in range(16)]
    mine = lax.all_to_all(spread, "ctx", 0, 0, axis_index_groups=groups)
    partner = lax.ppermute(kv, "ctx", swap)

    smem = pl.BlockSpec(memory_space=pltpu.SMEM)
    vmem = pl.BlockSpec(memory_space=pltpu.VMEM)
    params = pltpu.CompilerParams(vmem_limit_bytes=VMEM_LIMIT)
    wide = jax.ShapeDtypeStruct((rows, HEAD), jnp.float32)
    holds = [pltpu.VMEM((rows, CHUNK), jnp.float32)] * 2
    best, total, acc = pl.pallas_call(
        local_kernel,
        out_shape=(wide, wide, wide),
        in_specs=[smem, vmem, vmem, vmem],
        out_specs=(vmem, vmem, vmem),
        scratch_shapes=[pltpu.VMEM((rows, HEAD), jnp.int32)],
        compiler_params=params,
        cost_estimate=pl.CostEstimate(
            flops=6 * rows * CHUNK * HEAD * 4, bytes_accessed=2**24, transcendentals=0
        ),
    )(doc_lengths, q, kv, partner)
    mine, best, total, acc = lax.optimization_barrier((mine, best, total, acc))
    theirs = lax.ppermute(mine, "ctx", swap)
    best, total, acc = pl.pallas_call(
        middle_kernel,
        out_shape=(wide, wide, wide),
        in_specs=[smem] + [vmem] * 5,
        out_specs=(vmem, vmem, vmem),
        scratch_shapes=holds,
        compiler_params=params,
        cost_estimate=pl.CostEstimate(
            flops=14 * rows * CHUNK * HEAD * 4, bytes_accessed=2**24, transcendentals=0
        ),
    )(doc_lengths, q, mine, best, total, acc)
    out = pl.pallas_call(
        last_kernel,
        out_shape=jax.ShapeDtypeStruct((rows, HEAD), jnp.bfloat16),
        in_specs=[smem] + [vmem] * 5,
        out_specs=vmem,
        scratch_shapes=[pltpu.VMEM((rows, HEAD), jnp.float32)] * 3 + holds,
        compiler_params=params,
        cost_estimate=pl.CostEstimate(
            flops=14 * rows * CHUNK * HEAD * 4, bytes_accessed=2**24, transcendentals=0
        ),
    )(doc_lengths, q, theirs, best, total, acc)
    return out.reshape(queries.shape)


def solution(mesh):
    placed = (
        P(("dp", "ctx"), "tp", None),
        P(("dp", "ctx"), "tp", None),
        P(("dp", "ctx"), "tp", None),
        P("dp"),
    )
    return jax.shard_map(
        per_device,
        mesh=mesh,
        in_specs=placed,
        out_specs=P(("dp", "ctx"), "tp", None),
        check_vma=False,
    )
```

time: 42 us -> 41.6 us (level)
  the two profiles are of different devices: /device:TPU:415 before, /device:TPU:14 now
where the time goes in v2:
time: 41.6 us; the launch traced here: 41.3 us
  Pallas kernels  17.6 us (42%)
  starting transfers between devices  15 us (36%)
  local copies, waits for them, and re-layouts  5.6 us (13%)
  waiting for transfers between devices  2.07 us (5%)
  other arithmetic  0.9 us (2%)
    all_to_all x1, starting transfers between devices, per_device(): mine = lax.all_to_all(spread, 'ctx', 0, 0, axis_index_groups=groups)  9.37 us
    pallas_call x1, Pallas kernels, per_device(): pl.pallas_call(last_kernel, out_shape=jax.ShapeDtypeStruct((rows, HEAD),...  7.44 us
    pallas_call x1, Pallas kernels, per_device(): pl.pallas_call(middle_kernel, out_shape=(wide, wide, wide), in_specs=[sme...  6.6 us
    unnamed x16, local copies, waits for them, and re-layouts  4.42 us
    ppermute x1, starting transfers between devices, per_device(): theirs = lax.ppermute(mine, 'ctx', swap)  3.75 us
    pallas_call x1, Pallas kernels, per_device(): pl.pallas_call(local_kernel, out_shape=(wide, wide, wide), in_specs=[smem...  3.55 us
    ppermute x1, starting transfers between devices, per_device(): partner = lax.ppermute(kv, 'ctx', swap)  1.92 us
    ppermute x1, waiting for transfers between devices, per_device(): partner = lax.ppermute(kv, 'ctx', swap)  1.31 us
  transfers between devices with their start and end apart: 3, of which 2 were waited for; matrix products, arithmetic and copies ran while one was open for 0% of the time, Pallas kernels for 25%

profile of v2, /device:TPU:14, one launch (start us, length us, event | category | flops | bytes accessed | tf_op | source)
XLA Modules:
  0.0 41.3 jit_solution(5623632579671734857)
XLA Ops:
  0.0 0.9 %pad_maximum_fusion = bf16[2,256,128]{2,1,0:T(8,128)(2,1)S(1)} fusion(bf16[1,256,128]{2,1,0:T(8,128)(2,1)} %bitcast.9, bf16[1,256,128]{2,1,0:T(8,128)(2,1)} %bitcast.11), kind=kLoop, calls=%fused_computation | loop fusion | flops 65536 | bytes 262144 | tf_op jit(solution)/shard_map/stack | solution.py:191
  0.9 1.2 %broadcast_in_dim.2 = bf16[8,2,256,128]{3,2,1,0:T(8,128)(2,1)} broadcast(bf16[2,256,128]{2,1,0:T(8,128)(2,1)S(1)} %pad_maximum_fusion), dimensions={1,2,3} | broadcast | bytes 1179648 | tf_op jit(solution)/shard_map/broadcast_in_dim | solution.py:190
  2.1 0.0 copy-start.6
  2.1 0.0 copy-start.7
  2.1 0.0 copy-start
  2.1 9.4 %all-to-all-start = ((bf16[8,2,256,128]{3,2,1,0:T(8,128)(2,1)}), bf16[8,2,256,128]{3,2,1,0:T(8,128)(2,1)S(1)}, u32[]{:S(2)}, u32[]{:S(2)}) async-start(bf16[8,2,256,128]{3,2,1,0:T(8,128)(2,1)} %broadcast_in_dim.2), calls=%async_computation | async-start | bytes 2097152 | tf_op jit(solution)/shard_map/all_to_all | solution.py:197
  11.4 0.0 copy-done.6
  11.4 0.0 copy-done.7
  11.5 0.0 copy-start.1
  11.5 1.9 %collective-permute-start = (bf16[2,256,128]{2,1,0:T(8,128)(2,1)S(1)}, bf16[2,256,128]{2,1,0:T(8,128)(2,1)S(1)}, u32[]{:S(2)}, u32[]{:S(2)}) collective-permute-start(bf16[2,256,128]{2,1,0:T(8,128)(2,1)S(1)} %pad_maximum_fusion.1.own), channel_id=1, source_target_pairs={{0,8},{8,0},{16,24},{24,16},{32,40},{40,32},{48,56},{56,48},{64,72... | collective-permute-start | bytes 393224 | tf_op jit(solution)/shard_map/ppermute | solution.py:198
  13.4 1.3 %collective-permute-done.partner = bf16[2,256,128]{2,1,0:T(8,128)(2,1)S(1)} collective-permute-done((bf16[2,256,128]{2,1,0:T(8,128)(2,1)S(1)}, bf16[2,256,128]{2,1,0:T(8,128)(2,1)S(1)}, u32[]{:S(2)}, u32[]{:S(2)}) %collective-permute-start) | collective-permute-done | bytes 131104 | tf_op jit(solution)/shard_map/ppermute | solution.py:198
  14.7 0.0 copy-done
  14.7 0.0 copy-done.1
  14.7 3.6 %shard_map.46 = (f32[2048,128]{1,0:T(8,128)S(1)}, f32[2048,128]{1,0:T(8,128)S(1)}, f32[2048,128]{1,0:T(8,128)S(1)}) custom-call(s32[12]{0:T(128)S(1)} %copy-done.1, bf16[2048,128]{1,0:T(8,128)(2,1)S(1)} %bitcast.6, bf16[2,256,128]{2,1,0:T(8,128)(2,1)S(1)} %pad_maximum_fusion.1.own, bf16[2,256,128]{2,1,0:T(8,128)(2,1)S(1)} %collective-permute-done.partner), custom_call_target="tpu_custom_call" | custom-call | flops 1610612736 | bytes 16777216 | tf_op jit(solution)/shard_map/pallas_call | solution.py:205
  18.3 0.0 copy-start.2
  18.3 1.0 %copy-done.2 = f32[2048,128]{1,0:T(8,128)} copy-done((f32[2048,128]{1,0:T(8,128)}, f32[2048,128]{1,0:T(8,128)S(1)}, u32[]{:S(2)}) %copy-start.2) | copy-done | bytes 1048600
  19.3 0.0 copy-start.4
  19.3 1.0 %copy-done.4 = f32[2048,128]{1,0:T(8,128)} copy-done((f32[2048,128]{1,0:T(8,128)}, f32[2048,128]{1,0:T(8,128)S(1)}, u32[]{:S(2)}) %copy-start.4) | copy-done | bytes 1048600
  20.3 0.7 %all-to-all-done.kv = bf16[8,2,256,128]{3,2,1,0:T(8,128)(2,1)S(1)} async-done(((bf16[8,2,256,128]{3,2,1,0:T(8,128)(2,1)}), bf16[8,2,256,128]{3,2,1,0:T(8,128)(2,1)S(1)}, u32[]{:S(2)}, u32[]{:S(2)}) %all-to-all-start) | async-done | bytes 1048608 | tf_op jit(solution)/shard_map/all_to_all | solution.py:197
  21.0 3.7 %collective-permute-start.1 = (bf16[8,2,256,128]{3,2,1,0:T(8,128)(2,1)S(1)}, bf16[8,2,256,128]{3,2,1,0:T(8,128)(2,1)S(1)}, u32[]{:S(2)}, u32[]{:S(2)}) collective-permute-start(bf16[8,2,256,128]{3,2,1,0:T(8,128)(2,1)S(1)} %all-to-all-done.kv), channel_id=1, source_target_pairs={{0,8},{8,0},{16,24},{24,16},{32,40},{40,32},{48,56},{56,48},{64,72... | collective-permute-start | bytes 3145736 | tf_op jit(solution)/shard_map/ppermute | solution.py:217
  24.8 0.0 copy-start.3
  24.8 1.2 %copy-done.3 = f32[2048,128]{1,0:T(8,128)S(1)} copy-done((f32[2048,128]{1,0:T(8,128)S(1)}, f32[2048,128]{1,0:T(8,128)}, u32[]{:S(2)}) %copy-start.3) | copy-done | bytes 1048600
  26.0 0.0 copy-start.5
  26.0 1.2 %copy-done.5 = f32[2048,128]{1,0:T(8,128)S(1)} copy-done((f32[2048,128]{1,0:T(8,128)S(1)}, f32[2048,128]{1,0:T(8,128)}, u32[]{:S(2)}) %copy-start.5) | copy-done | bytes 1048600
  27.2 6.6 %shard_map.47 = (f32[2048,128]{1,0:T(8,128)S(1)}, f32[2048,128]{1,0:T(8,128)S(1)}, f32[2048,128]{1,0:T(8,128)S(1)}) custom-call(s32[12]{0:T(128)S(1)} %copy-done.1, bf16[2048,128]{1,0:T(8,128)(2,1)S(1)} %bitcast.7, bf16[8,2,256,128]{3,2,1,0:T(8,128)(2,1)S(1)} %all-to-all-done.kv, f32[2048,128]{1,0:T(8,128)S(1)} %get-tuple-element.23.best_in, ...), custom_call_target="tpu_custom_call" | custom-call | flops 3758096384 | bytes 16777216 | tf_op jit(solution)/shard_map/pallas_call | solution.py:218
  33.8 0.0 collective-permute-done.1.kv
  33.8 7.4 %shard_map.48 = bf16[2048,128]{1,0:T(8,128)(2,1)} custom-call(s32[12]{0:T(128)S(1)} %copy-done.1, bf16[2048,128]{1,0:T(8,128)(2,1)S(1)} %bitcast.8, bf16[8,2,256,128]{3,2,1,0:T(8,128)(2,1)S(1)} %collective-permute-done.1.kv, f32[2048,128]{1,0:T(8,128)S(1)} %get-tuple-element.26.best_in, f32[2048,128]{1,0:T(8,128)S(1)} %get-tuple-element.27.total_in, ...), custom_call_target="tpu_custom_call" | custom-call | flops 3758096384 | bytes 16777216 | tf_op jit(solution)/shard_map/pallas_call | solution.py:229
  (1 shorter events, 0.0 us)
Async XLA Ops:
  2.1 9.4 %copy-start.6 = (bf16[256,1,128]{2,0,1:T(8,128)(2,1)S(1)}, bf16[256,1,128]{2,0,1:T(8,128)(2,1)}, u32[]{:S(2)}) copy-start(bf16[256,1,128]{2,0,1:T(8,128)(2,1)} %param.6) | copy-start | bytes 196612
  2.1 9.4 %copy-start.7 = (bf16[256,1,128]{2,0,1:T(8,128)(2,1)S(1)}, bf16[256,1,128]{2,0,1:T(8,128)(2,1)}, u32[]{:S(2)}) copy-start(bf16[256,1,128]{2,0,1:T(8,128)(2,1)} %param.5) | copy-start | bytes 196612
  2.1 12.7 %copy-start = (bf16[256,8,128]{2,1,0:T(8,128)(2,1)S(1)}, bf16[256,8,128]{2,1,0:T(8,128)(2,1)}, u32[]{:S(2)}) copy-start(bf16[256,8,128]{2,1,0:T(8,128)(2,1)} %param.4) | copy-start | bytes 1572868
  2.1 18.9 %all-to-all-start = ((bf16[8,2,256,128]{3,2,1,0:T(8,128)(2,1)}), bf16[8,2,256,128]{3,2,1,0:T(8,128)(2,1)S(1)}, u32[]{:S(2)}, u32[]{:S(2)}) async-start(bf16[8,2,256,128]{3,2,1,0:T(8,128)(2,1)} %broadcast_in_dim.2), calls=%async_computation | async-start | bytes 2097152 | tf_op jit(solution)/shard_map/all_to_all | solution.py:197
  11.5 3.3 %copy-start.1 = (s32[12]{0:T(128)S(1)}, s32[12]{0:T(128)}, u32[]{:S(2)}) copy-start(s32[12]{0:T(128)} %lengths.5) | copy-start | bytes 148
  11.5 3.2 %collective-permute-start = (bf16[2,256,128]{2,1,0:T(8,128)(2,1)S(1)}, bf16[2,256,128]{2,1,0:T(8,128)(2,1)S(1)}, u32[]{:S(2)}, u32[]{:S(2)}) collective-permute-start(bf16[2,256,128]{2,1,0:T(8,128)(2,1)S(1)} %pad_maximum_fusion.1.own), channel_id=1, source_target_pairs={{0,8},{8,0},{16,24},{24,16},{32,40},{40,32},{48,56},{56,48},{64,72... | collective-permute-start | bytes 393224 | tf_op jit(solution)/shard_map/ppermute | solution.py:198
  18.3 1.0 %copy-start.2 = (f32[2048,128]{1,0:T(8,128)}, f32[2048,128]{1,0:T(8,128)S(1)}, u32[]{:S(2)}) copy-start(f32[2048,128]{1,0:T(8,128)S(1)} %get-tuple-element.24.total_in) | copy-start | bytes 3145732
  19.3 1.0 %copy-start.4 = (f32[2048,128]{1,0:T(8,128)}, f32[2048,128]{1,0:T(8,128)S(1)}, u32[]{:S(2)}) copy-start(f32[2048,128]{1,0:T(8,128)S(1)} %get-tuple-element.25.acc_in) | copy-start | bytes 3145732
  21.0 12.8 %collective-permute-start.1 = (bf16[8,2,256,128]{3,2,1,0:T(8,128)(2,1)S(1)}, bf16[8,2,256,128]{3,2,1,0:T(8,128)(2,1)S(1)}, u32[]{:S(2)}, u32[]{:S(2)}) collective-permute-start(bf16[8,2,256,128]{3,2,1,0:T(8,128)(2,1)S(1)} %all-to-all-done.kv), channel_id=1, source_target_pairs={{0,8},{8,0},{16,24},{24,16},{32,40},{40,32},{48,56},{56,48},{64,72... | collective-permute-start | bytes 3145736 | tf_op jit(solution)/shard_map/ppermute | solution.py:217
  24.8 1.2 %copy-start.3 = (f32[2048,128]{1,0:T(8,128)S(1)}, f32[2048,128]{1,0:T(8,128)}, u32[]{:S(2)}) copy-start(f32[2048,128]{1,0:T(8,128)} %copy-done.2) | copy-start | bytes 3145732
  26.0 1.2 %copy-start.5 = (f32[2048,128]{1,0:T(8,128)S(1)}, f32[2048,128]{1,0:T(8,128)}, u32[]{:S(2)}) copy-start(f32[2048,128]{1,0:T(8,128)} %copy-done.4) | copy-start | bytes 3145732

commit v3 on v2

--- a/solution.py
+++ b/solution.py
@@ -166,17 +166,36 @@
         lax.fori_loop(0, (hi - lo + 1) // 2, pair, stale)
 
 
-def middle_kernel(
-    lengths, q, kv, best_in, total_in, acc_in, best, total, acc, here, there
+def middle_kernel(lengths, q, kv, near_best, best, total, acc, here, there):
+    best[...] = near_best[...]
+    total[...] = jnp.zeros(total.shape, jnp.float32)
+    acc[...] = jnp.zeros(acc.shape, jnp.float32)
+    fold_chunks(lengths, q, kv, best, total, acc, here, there, True)
+
+
+def last_kernel(
+    lengths,
+    q,
+    kv,
+    near_best,
+    near_total,
+    near_acc,
+    best_in,
+    total_in,
+    acc_in,
+    out,
+    best,
+    total,
+    acc,
+    here,
+    there,
 ):
-    best[...], total[...], acc[...] = best_in[...], total_in[...], acc_in[...]
-    fold_chunks(lengths, q, kv, best, total, acc, here, there, True)
-
-
-def last_kernel(
-    lengths, q, kv, best_in, total_in, acc_in, out, best, total, acc, here, there
-):
-    best[...], total[...], acc[...] = best_in[...], total_in[...], acc_in[...]
+    for r in range(0, out.shape[0], BLOCK):
+        rs = slice(r, r + BLOCK)
+        shrink = jnp.exp2((near_best[rs, :] - best_in[rs, :]) * LOG2_SCALE)
+        best[rs, :] = best_in[rs, :]
+        total[rs, :] = total_in[rs, :] + near_total[rs, :] * shrink
+        acc[rs, :] = acc_in[rs, :] + near_acc[rs, :] * shrink
     fold_chunks(lengths, q, kv, best, total, acc, here, there, False)
     for r in range(0, out.shape[0], BLOCK):
         rs = slice(r, r + BLOCK)
@@ -202,7 +221,7 @@
     params = pltpu.CompilerParams(vmem_limit_bytes=VMEM_LIMIT)
     wide = jax.ShapeDtypeStruct((rows, HEAD), jnp.float32)
     holds = [pltpu.VMEM((rows, CHUNK), jnp.float32)] * 2
-    best, total, acc = pl.pallas_call(
+    near = pl.pallas_call(
         local_kernel,
         out_shape=(wide, wide, wide),
         in_specs=[smem, vmem, vmem, vmem],
@@ -213,30 +232,30 @@
             flops=6 * rows * CHUNK * HEAD * 4, bytes_accessed=2**24, transcendentals=0
         ),
     )(doc_lengths, q, kv, partner)
-    mine, best, total, acc = lax.optimization_barrier((mine, best, total, acc))
+    mine, near_best = lax.optimization_barrier((mine, near[0]))
     theirs = lax.ppermute(mine, "ctx", swap)
-    best, total, acc = pl.pallas_call(
+    far = pl.pallas_call(
         middle_kernel,
         out_shape=(wide, wide, wide),
-        in_specs=[smem] + [vmem] * 5,
+        in_specs=[smem] + [vmem] * 3,
         out_specs=(vmem, vmem, vmem),
         scratch_shapes=holds,
         compiler_params=params,
         cost_estimate=pl.CostEstimate(
             flops=14 * rows * CHUNK * HEAD * 4, bytes_accessed=2**24, transcendentals=0
         ),
-    )(doc_lengths, q, mine, best, total, acc)
+    )(doc_lengths, q, mine, near_best)
     out = pl.pallas_call(
         last_kernel,
         out_shape=jax.ShapeDtypeStruct((rows, HEAD), jnp.bfloat16),
-        in_specs=[smem] + [vmem] * 5,
+        in_specs=[smem] + [vmem] * 8,
         out_specs=vmem,
         scratch_shapes=[pltpu.VMEM((rows, HEAD), jnp.float32)] * 3 + holds,
         compiler_params=params,
         cost_estimate=pl.CostEstimate(
             flops=14 * rows * CHUNK * HEAD * 4, bytes_accessed=2**24, transcendentals=0
         ),
-    )(doc_lengths, q, theirs, best, total, acc)
+    )(doc_lengths, q, theirs, *near, *far)
     return out.reshape(queries.shape)
 
 

time: 41.6 us -> 38.4 us (0.923)
  the two profiles are of different devices: /device:TPU:14 before, /device:TPU:15 now
where the time goes in v3:
time: 38.4 us; the launch traced here: 38.2 us
  Pallas kernels  19 us (49%)
  starting transfers between devices  14 us (36%)
  local copies, waits for them, and re-layouts  3.17 us (8%)
  waiting for transfers between devices  0.97 us (3%)
  other arithmetic  0.9 us (2%)
    pallas_call x1, Pallas kernels, per_device(): pl.pallas_call(last_kernel, out_shape=jax.ShapeDtypeStruct((rows, HEAD),...  6.83 us
    ppermute x1, starting transfers between devices, per_device(): partner = lax.ppermute(kv, 'ctx', swap)  6.71 us
    pallas_call x1, Pallas kernels, per_device(): pl.pallas_call(middle_kernel, out_shape=(wide, wide, wide), in_specs=[sme...  6.21 us
    pallas_call x1, Pallas kernels, per_device(): pl.pallas_call(local_kernel, out_shape=(wide, wide, wide), in_specs=[smem...  6 us
    all_to_all x1, starting transfers between devices, per_device(): mine = lax.all_to_all(spread, 'ctx', 0, 0, axis_index_groups=groups)  5.25 us
    ppermute x1, starting transfers between devices, per_device(): theirs = lax.ppermute(mine, 'ctx', swap)  2.04 us
    unnamed x16, local copies, waits for them, and re-layouts  1.99 us
    broadcast_in_dim x1, local copies, waits for them, and re-layouts, per_device(): jnp.broadcast_to(jnp.stack([keys[:, 0], values[:, 0]])[None], (8, 2, toke...  1.18 us
  transfers between devices with their start and end apart: 3, of which 1 were waited for; matrix products, arithmetic and copies ran while one was open for 0% of the time, Pallas kernels for 32%

profile of v3, /device:TPU:15, one launch (start us, length us, event | category | flops | bytes accessed | tf_op | source)
XLA Modules:
  0.0 38.2 jit_solution(17564452307047148770)
XLA Ops:
  0.0 0.9 %pad_maximum_fusion = bf16[2,256,128]{2,1,0:T(8,128)(2,1)S(1)} fusion(bf16[1,256,128]{2,1,0:T(8,128)(2,1)} %bitcast.9, bf16[1,256,128]{2,1,0:T(8,128)(2,1)} %bitcast.11), kind=kLoop, calls=%fused_computation | loop fusion | flops 65536 | bytes 262144 | tf_op jit(solution)/shard_map/stack | solution.py:210
  0.9 1.2 %broadcast_in_dim.2 = bf16[8,2,256,128]{3,2,1,0:T(8,128)(2,1)} broadcast(bf16[2,256,128]{2,1,0:T(8,128)(2,1)S(1)} %pad_maximum_fusion), dimensions={1,2,3} | broadcast | bytes 1179648 | tf_op jit(solution)/shard_map/broadcast_in_dim | solution.py:209
  2.1 0.0 copy-start.6
  2.1 0.0 copy-start.7
  2.1 0.0 copy-start
  2.1 5.2 %all-to-all-start = ((bf16[8,2,256,128]{3,2,1,0:T(8,128)(2,1)}), bf16[8,2,256,128]{3,2,1,0:T(8,128)(2,1)S(1)}, u32[]{:S(2)}, u32[]{:S(2)}) async-start(bf16[8,2,256,128]{3,2,1,0:T(8,128)(2,1)} %broadcast_in_dim.2), calls=%async_computation | async-start | bytes 2097152 | tf_op jit(solution)/shard_map/all_to_all | solution.py:216
  7.3 0.0 copy-done.6
  7.3 0.0 copy-done.7
  7.3 0.0 copy-start.1
  7.4 6.7 %collective-permute-start = (bf16[2,256,128]{2,1,0:T(8,128)(2,1)S(1)}, bf16[2,256,128]{2,1,0:T(8,128)(2,1)S(1)}, u32[]{:S(2)}, u32[]{:S(2)}) collective-permute-start(bf16[2,256,128]{2,1,0:T(8,128)(2,1)S(1)} %pad_maximum_fusion.1.own), channel_id=1, source_target_pairs={{0,8},{8,0},{16,24},{24,16},{32,40},{40,32},{48,56},{56,48},{64,72... | collective-permute-start | bytes 393224 | tf_op jit(solution)/shard_map/ppermute | solution.py:217
  14.1 1.0 %collective-permute-done.partner = bf16[2,256,128]{2,1,0:T(8,128)(2,1)S(1)} collective-permute-done((bf16[2,256,128]{2,1,0:T(8,128)(2,1)S(1)}, bf16[2,256,128]{2,1,0:T(8,128)(2,1)S(1)}, u32[]{:S(2)}, u32[]{:S(2)}) %collective-permute-start) | collective-permute-done | bytes 131104 | tf_op jit(solution)/shard_map/ppermute | solution.py:217
  15.0 0.0 copy-done
  15.0 0.0 copy-done.1
  15.0 6.0 %shard_map.46 = (f32[2048,128]{1,0:T(8,128)S(1)}, f32[2048,128]{1,0:T(8,128)S(1)}, f32[2048,128]{1,0:T(8,128)S(1)}) custom-call(s32[12]{0:T(128)S(1)} %copy-done.1, bf16[2048,128]{1,0:T(8,128)(2,1)S(1)} %bitcast.6, bf16[2,256,128]{2,1,0:T(8,128)(2,1)S(1)} %pad_maximum_fusion.1.own, bf16[2,256,128]{2,1,0:T(8,128)(2,1)S(1)} %collective-permute-done.partner), custom_call_target="tpu_custom_call" | custom-call | flops 1610612736 | bytes 16777216 | tf_op jit(solution)/shard_map/pallas_call | solution.py:224
  21.0 0.0 copy-start.2
  21.1 1.0 %copy-done.2 = f32[2048,128]{1,0:T(8,128)} copy-done((f32[2048,128]{1,0:T(8,128)}, f32[2048,128]{1,0:T(8,128)S(1)}, u32[]{:S(2)}) %copy-start.2) | copy-done | bytes 1048600
  22.1 0.0 copy-start.4
  22.1 1.0 %copy-done.4 = f32[2048,128]{1,0:T(8,128)} copy-done((f32[2048,128]{1,0:T(8,128)}, f32[2048,128]{1,0:T(8,128)S(1)}, u32[]{:S(2)}) %copy-start.4) | copy-done | bytes 1048600
  23.0 0.0 all-to-all-done.kv
  23.0 0.0 copy-start.3
  23.0 0.0 copy-start.5
  23.0 2.0 %collective-permute-start.1 = (bf16[8,2,256,128]{3,2,1,0:T(8,128)(2,1)S(1)}, bf16[8,2,256,128]{3,2,1,0:T(8,128)(2,1)S(1)}, u32[]{:S(2)}, u32[]{:S(2)}) collective-permute-start(bf16[8,2,256,128]{3,2,1,0:T(8,128)(2,1)S(1)} %all-to-all-done.kv), channel_id=1, source_target_pairs={{0,8},{8,0},{16,24},{24,16},{32,40},{40,32},{48,56},{56,48},{64,72... | collective-permute-start | bytes 3145736 | tf_op jit(solution)/shard_map/ppermute | solution.py:236
  25.1 6.2 %shard_map.47 = (f32[2048,128]{1,0:T(8,128)S(1)}, f32[2048,128]{1,0:T(8,128)S(1)}, f32[2048,128]{1,0:T(8,128)S(1)}) custom-call(s32[12]{0:T(128)S(1)} %copy-done.1, bf16[2048,128]{1,0:T(8,128)(2,1)S(1)} %bitcast.7, bf16[8,2,256,128]{3,2,1,0:T(8,128)(2,1)S(1)} %all-to-all-done.kv, f32[2048,128]{1,0:T(8,128)S(1)} %get-tuple-element.21.near_best), custom_call_target="tpu_custom_call" | custom-call | flops 3758096384 | bytes 16777216 | tf_op jit(solution)/shard_map/pallas_call | solution.py:237
  31.3 0.0 collective-permute-done.1.kv
  31.3 0.0 copy-done.3
  31.3 0.0 copy-done.5
  31.3 6.8 %shard_map.48 = bf16[2048,128]{1,0:T(8,128)(2,1)} custom-call(s32[12]{0:T(128)S(1)} %copy-done.1, bf16[2048,128]{1,0:T(8,128)(2,1)S(1)} %bitcast.8, bf16[8,2,256,128]{3,2,1,0:T(8,128)(2,1)S(1)} %collective-permute-done.1.kv, f32[2048,128]{1,0:T(8,128)S(1)} %get-tuple-element.21.near_best, f32[2048,128]{1,0:T(8,128)S(1)} %copy-done.3, ...), custom_call_target="tpu_custom_call" | custom-call | flops 3758096384 | bytes 16777216 | tf_op jit(solution)/shard_map/pallas_call | solution.py:248
  (1 shorter events, 0.0 us)
Async XLA Ops:
  2.1 5.3 %copy-start.6 = (bf16[256,1,128]{2,0,1:T(8,128)(2,1)S(1)}, bf16[256,1,128]{2,0,1:T(8,128)(2,1)}, u32[]{:S(2)}) copy-start(bf16[256,1,128]{2,0,1:T(8,128)(2,1)} %param.6) | copy-start | bytes 196612
  2.1 5.3 %copy-start.7 = (bf16[256,1,128]{2,0,1:T(8,128)(2,1)S(1)}, bf16[256,1,128]{2,0,1:T(8,128)(2,1)}, u32[]{:S(2)}) copy-start(bf16[256,1,128]{2,0,1:T(8,128)(2,1)} %param.5) | copy-start | bytes 196612
  2.1 13.0 %copy-start = (bf16[256,8,128]{2,1,0:T(8,128)(2,1)S(1)}, bf16[256,8,128]{2,1,0:T(8,128)(2,1)}, u32[]{:S(2)}) copy-start(bf16[256,8,128]{2,1,0:T(8,128)(2,1)} %param.4) | copy-start | bytes 1572868
  2.1 21.0 %all-to-all-start = ((bf16[8,2,256,128]{3,2,1,0:T(8,128)(2,1)}), bf16[8,2,256,128]{3,2,1,0:T(8,128)(2,1)S(1)}, u32[]{:S(2)}, u32[]{:S(2)}) async-start(bf16[8,2,256,128]{3,2,1,0:T(8,128)(2,1)} %broadcast_in_dim.2), calls=%async_computation | async-start | bytes 2097152 | tf_op jit(solution)/shard_map/all_to_all | solution.py:216
  7.3 7.7 %copy-start.1 = (s32[12]{0:T(128)S(1)}, s32[12]{0:T(128)}, u32[]{:S(2)}) copy-start(s32[12]{0:T(128)} %lengths.5) | copy-start | bytes 148
  7.4 7.7 %collective-permute-start = (bf16[2,256,128]{2,1,0:T(8,128)(2,1)S(1)}, bf16[2,256,128]{2,1,0:T(8,128)(2,1)S(1)}, u32[]{:S(2)}, u32[]{:S(2)}) collective-permute-start(bf16[2,256,128]{2,1,0:T(8,128)(2,1)S(1)} %pad_maximum_fusion.1.own), channel_id=1, source_target_pairs={{0,8},{8,0},{16,24},{24,16},{32,40},{40,32},{48,56},{56,48},{64,72... | collective-permute-start | bytes 393224 | tf_op jit(solution)/shard_map/ppermute | solution.py:217
  21.0 1.0 %copy-start.2 = (f32[2048,128]{1,0:T(8,128)}, f32[2048,128]{1,0:T(8,128)S(1)}, u32[]{:S(2)}) copy-start(f32[2048,128]{1,0:T(8,128)S(1)} %get-tuple-element.19.near_total) | copy-start | bytes 3145732
  22.1 1.0 %copy-start.4 = (f32[2048,128]{1,0:T(8,128)}, f32[2048,128]{1,0:T(8,128)S(1)}, u32[]{:S(2)}) copy-start(f32[2048,128]{1,0:T(8,128)S(1)} %get-tuple-element.20.near_acc) | copy-start | bytes 3145732
  23.0 8.3 %copy-start.3 = (f32[2048,128]{1,0:T(8,128)S(1)}, f32[2048,128]{1,0:T(8,128)}, u32[]{:S(2)}) copy-start(f32[2048,128]{1,0:T(8,128)} %copy-done.2) | copy-start | bytes 3145732
  23.0 8.3 %copy-start.5 = (f32[2048,128]{1,0:T(8,128)S(1)}, f32[2048,128]{1,0:T(8,128)}, u32[]{:S(2)}) copy-start(f32[2048,128]{1,0:T(8,128)} %copy-done.4) | copy-start | bytes 3145732
  23.0 8.3 %collective-permute-start.1 = (bf16[8,2,256,128]{3,2,1,0:T(8,128)(2,1)S(1)}, bf16[8,2,256,128]{3,2,1,0:T(8,128)(2,1)S(1)}, u32[]{:S(2)}, u32[]{:S(2)}) collective-permute-start(bf16[8,2,256,128]{3,2,1,0:T(8,128)(2,1)S(1)} %all-to-all-done.kv), channel_id=1, source_target_pairs={{0,8},{8,0},{16,24},{24,16},{32,40},{40,32},{48,56},{56,48},{64,72... | collective-permute-start | bytes 3145736 | tf_op jit(solution)/shard_map/ppermute | solution.py:236

commit v4 on v3

--- a/solution.py
+++ b/solution.py
@@ -14,6 +14,7 @@
 LOWEST = -1e30
 HIDDEN = 1e30
 SLACK = 40.0 / LOG2_SCALE
+REACH = 100.0 / LOG2_SCALE
 VMEM_LIMIT = 20 * 2**20
 
 
@@ -47,7 +48,7 @@
     return jnp.concatenate(done, 1)
 
 
-def local_kernel(lengths, q, own, partner, best, total, acc, starts):
+def local_kernel(lengths, q, own, partner, best, total, acc, reach, starts):
     rows = q.shape[0]
     group = rows // CHUNK
     position, first, first_start, begins = place(lengths)
@@ -86,10 +87,21 @@
         fold(partner, position - 1)
 
     fold(own, position)
-    best[...] = jnp.where(starts[...] == first_start, best[...], HIDDEN)
-
-
-def fold_chunks(lengths, q, kv, best, total, acc, here, there, mine):
+    longest = jnp.zeros((8, HEAD), jnp.float32)
+    least = jnp.full((8, HEAD), HIDDEN, jnp.float32)
+    for r in range(0, rows, BLOCK):
+        rs = slice(r, r + BLOCK)
+        kept = jnp.where(starts[rs, :] == first_start, best[rs, :], HIDDEN)
+        best[rs, :] = kept
+        least = jnp.minimum(least, jnp.min(kept.reshape(BLOCK // 8, 8, HEAD), axis=0))
+        squares = jnp.square(q[rs, :].astype(jnp.float32))
+        norms = jnp.broadcast_to(jnp.sum(squares, axis=1, keepdims=True), squares.shape)
+        longest = jnp.maximum(longest, jnp.max(norms.reshape(BLOCK // 8, 8, HEAD), axis=0))
+    reach[0] = jnp.broadcast_to(jnp.max(longest, axis=0, keepdims=True), (8, HEAD))
+    reach[1] = jnp.broadcast_to(jnp.min(least, axis=0, keepdims=True), (8, HEAD))
+
+
+def fold_chunks(lengths, q, kv, reach, best, total, acc, here, there, mine):
     rows = q.shape[0]
     position, _, first_start, _ = place(lengths)
     core = lax.rem(position, 2)
@@ -149,28 +161,86 @@
             acc[rs, :] += jnp.dot(low, kv[tile, 1], preferred_element_type=jnp.float32)
         return flag_of(over)
 
+    def fast(tile, count):
+        lane = lax.broadcasted_iota(jnp.int32, (1, CHUNK), 1)
+        keys = [(2 * (tile + i) + core) * CHUNK + lane for i in range(count)]
+        seen = [(key >= first_start) & (key < hi * 2 * CHUNK) for key in keys]
+
+        def score(r):
+            return [
+                jnp.where(seen[i], scores(q[r : r + BLOCK, :], kv[tile + i, 0]), LOWEST)
+                for i in range(count)
+            ]
+
+        def add(r, low):
+            acc[r : r + BLOCK, :] += sum(
+                jnp.dot(part, kv[tile + i, 1], preferred_element_type=jnp.float32)
+                for i, part in enumerate(low)
+            )
+
+        s = score(0)
+        waiting = None
+        for r in range(0, rows, BLOCK):
+            later = score(r + BLOCK) if r + BLOCK < rows else None
+            if waiting is not None:
+                add(*waiting)
+            rs = slice(r, r + BLOCK)
+            base = best[rs, :] * LOG2_SCALE
+            weights = [
+                [jnp.exp2(part * LOG2_SCALE - base) for part in split(block)] for block in s
+            ]
+            total[rs, :] += sum(w for row in weights for w in row)
+            low = [jnp.concatenate([w.astype(jnp.bfloat16) for w in row], 1) for row in weights]
+            waiting, s = (r, low), later
+        add(*waiting)
+
     @pl.when(lo < hi)
     def _():
-        stale = first_scores()
-
-        def pair(i, stale):
-            tile = lo + 2 * i
-            stale = step(tile, here, there, stale)
-            return lax.cond(
-                tile + 1 < hi,
-                lambda flag: step(tile + 1, there, here, flag),
-                lambda flag: flag,
-                stale,
-            )
-
-        lax.fori_loop(0, (hi - lo + 1) // 2, pair, stale)
-
-
-def middle_kernel(lengths, q, kv, near_best, best, total, acc, here, there):
+        peak = jnp.zeros((8, HEAD), jnp.float32)
+        for i in range(kv.shape[0]):
+            size = jnp.abs(kv[i, 0].astype(jnp.float32))
+            peak = jnp.maximum(peak, jnp.max(size.reshape(CHUNK // 8, 8, HEAD), axis=0))
+        peak = jnp.max(peak, axis=0, keepdims=True)
+        size = jnp.sum(jnp.square(peak), axis=1, keepdims=True)
+        bound = jnp.sqrt(size * reach[0, :1]) * 1.01 - reach[1, :1]
+        near = jnp.max(bound) < REACH
+
+        @pl.when(near)
+        def _():
+            count = hi - lo
+
+            def pair(i, carry):
+                fast(lo + 2 * i, 2)
+                return carry
+
+            lax.fori_loop(0, count // 2, pair, 0)
+
+            @pl.when(lax.rem(count, 2) == 1)
+            def _():
+                fast(hi - 1, 1)
+
+        @pl.when(jnp.logical_not(near))
+        def _():
+            stale = first_scores()
+
+            def pair(i, stale):
+                tile = lo + 2 * i
+                stale = step(tile, here, there, stale)
+                return lax.cond(
+                    tile + 1 < hi,
+                    lambda flag: step(tile + 1, there, here, flag),
+                    lambda flag: flag,
+                    stale,
+                )
+
+            lax.fori_loop(0, (hi - lo + 1) // 2, pair, stale)
+
+
+def middle_kernel(lengths, q, kv, reach, near_best, best, total, acc, here, there):
     best[...] = near_best[...]
     total[...] = jnp.zeros(total.shape, jnp.float32)
     acc[...] = jnp.zeros(acc.shape, jnp.float32)
-    fold_chunks(lengths, q, kv, best, total, acc, here, there, True)
+    fold_chunks(lengths, q, kv, reach, best, total, acc, here, there, True)
 
 
 def last_kernel(
@@ -180,6 +250,7 @@
     near_best,
     near_total,
     near_acc,
+    reach,
     best_in,
     total_in,
     acc_in,
@@ -196,7 +267,7 @@
         best[rs, :] = best_in[rs, :]
         total[rs, :] = total_in[rs, :] + near_total[rs, :] * shrink
         acc[rs, :] = acc_in[rs, :] + near_acc[rs, :] * shrink
-    fold_chunks(lengths, q, kv, best, total, acc, here, there, False)
+    fold_chunks(lengths, q, kv, reach, best, total, acc, here, there, False)
     for r in range(0, out.shape[0], BLOCK):
         rs = slice(r, r + BLOCK)
         out[rs, :] = (acc[rs, :] / jnp.sum(total[rs, :], axis=1, keepdims=True)).astype(out.dtype)
@@ -223,9 +294,9 @@
     holds = [pltpu.VMEM((rows, CHUNK), jnp.float32)] * 2
     near = pl.pallas_call(
         local_kernel,
-        out_shape=(wide, wide, wide),
+        out_shape=(wide, wide, wide, jax.ShapeDtypeStruct((2, 8, HEAD), jnp.float32)),
         in_specs=[smem, vmem, vmem, vmem],
-        out_specs=(vmem, vmem, vmem),
+        out_specs=(vmem, vmem, vmem, vmem),
         scratch_shapes=[pltpu.VMEM((rows, HEAD), jnp.int32)],
         compiler_params=params,
         cost_estimate=pl.CostEstimate(
@@ -237,18 +308,18 @@
     far = pl.pallas_call(
         middle_kernel,
         out_shape=(wide, wide, wide),
-        in_specs=[smem] + [vmem] * 3,
+        in_specs=[smem] + [vmem] * 4,
         out_specs=(vmem, vmem, vmem),
         scratch_shapes=holds,
         compiler_params=params,
         cost_estimate=pl.CostEstimate(
             flops=14 * rows * CHUNK * HEAD * 4, bytes_accessed=2**24, transcendentals=0
         ),
-    )(doc_lengths, q, mine, near_best)
+    )(doc_lengths, q, mine, near[3], near_best)
     out = pl.pallas_call(
         last_kernel,
         out_shape=jax.ShapeDtypeStruct((rows, HEAD), jnp.bfloat16),
-        in_specs=[smem] + [vmem] * 8,
+        in_specs=[smem] + [vmem] * 9,
         out_specs=vmem,
         scratch_shapes=[pltpu.VMEM((rows, HEAD), jnp.float32)] * 3 + holds,
         compiler_params=params,

time: 38.4 us -> 40 us (1.042)
  the two profiles are of different devices: /device:TPU:15 before, /device:TPU:6 now
where the time goes in v4:
time: 40 us; the launch traced here: 39.8 us
  Pallas kernels  18.4 us (46%)
  starting transfers between devices  14.4 us (36%)
  local copies, waits for them, and re-layouts  3.17 us (8%)
  waiting for transfers between devices  2.77 us (7%)
  other arithmetic  0.9 us (2%)
    all_to_all x1, starting transfers between devices, per_device(): mine = lax.all_to_all(spread, 'ctx', 0, 0, axis_index_groups=groups)  9.48 us
    pallas_call x1, Pallas kernels, per_device(): pl.pallas_call(last_kernel, out_shape=jax.ShapeDtypeStruct((rows, HEAD),...  7.88 us
    pallas_call x1, Pallas kernels, per_device(): pl.pallas_call(middle_kernel, out_shape=(wide, wide, wide), in_specs=[sme...  6.8 us
    pallas_call x1, Pallas kernels, per_device(): pl.pallas_call(local_kernel, out_shape=(wide, wide, wide, jax.ShapeDtypeS...  3.74 us
    ppermute x1, starting transfers between devices, per_device(): theirs = lax.ppermute(mine, 'ctx', swap)  3.04 us
    unnamed x16, local copies, waits for them, and re-layouts  1.99 us
    ppermute x1, starting transfers between devices, per_device(): partner = lax.ppermute(kv, 'ctx', swap)  1.92 us
    all_to_all x1, waiting for transfers between devices, per_device(): mine = lax.all_to_all(spread, 'ctx', 0, 0, axis_index_groups=groups)  1.46 us
  transfers between devices with their start and end apart: 3, of which 2 were waited for; matrix products, arithmetic and copies ran while one was open for 0% of the time, Pallas kernels for 26%

profile of v4, /device:TPU:6, one launch (start us, length us, event | category | flops | bytes accessed | tf_op | source)
XLA Modules:
  0.0 39.8 jit_solution(9741501613567444080)
XLA Ops:
  0.0 0.9 %pad_maximum_fusion = bf16[2,256,128]{2,1,0:T(8,128)(2,1)S(1)} fusion(bf16[1,256,128]{2,1,0:T(8,128)(2,1)} %bitcast.9, bf16[1,256,128]{2,1,0:T(8,128)(2,1)} %bitcast.11), kind=kLoop, calls=%fused_computation | loop fusion | flops 65536 | bytes 262144 | tf_op jit(solution)/shard_map/stack | solution.py:281
  0.9 1.2 %broadcast_in_dim.2 = bf16[8,2,256,128]{3,2,1,0:T(8,128)(2,1)} broadcast(bf16[2,256,128]{2,1,0:T(8,128)(2,1)S(1)} %pad_maximum_fusion), dimensions={1,2,3} | broadcast | bytes 1179648 | tf_op jit(solution)/shard_map/broadcast_in_dim | solution.py:280
  2.1 0.0 copy-start.6
  2.1 0.0 copy-start.7
  2.1 0.0 copy-start
  2.1 9.5 %all-to-all-start = ((bf16[8,2,256,128]{3,2,1,0:T(8,128)(2,1)}), bf16[8,2,256,128]{3,2,1,0:T(8,128)(2,1)S(1)}, u32[]{:S(2)}, u32[]{:S(2)}) async-start(bf16[8,2,256,128]{3,2,1,0:T(8,128)(2,1)} %broadcast_in_dim.2), calls=%async_computation | async-start | bytes 2097152 | tf_op jit(solution)/shard_map/all_to_all | solution.py:287
  11.5 0.0 copy-done.6
  11.5 0.0 copy-done.7
  11.6 0.0 copy-start.1
  11.6 1.9 %collective-permute-start = (bf16[2,256,128]{2,1,0:T(8,128)(2,1)S(1)}, bf16[2,256,128]{2,1,0:T(8,128)(2,1)S(1)}, u32[]{:S(2)}, u32[]{:S(2)}) collective-permute-start(bf16[2,256,128]{2,1,0:T(8,128)(2,1)S(1)} %pad_maximum_fusion.1.own), channel_id=1, source_target_pairs={{0,8},{8,0},{16,24},{24,16},{32,40},{40,32},{48,56},{56,48},{64,72... | collective-permute-start | bytes 393224 | tf_op jit(solution)/shard_map/ppermute | solution.py:288
  13.5 1.3 %collective-permute-done.partner = bf16[2,256,128]{2,1,0:T(8,128)(2,1)S(1)} collective-permute-done((bf16[2,256,128]{2,1,0:T(8,128)(2,1)S(1)}, bf16[2,256,128]{2,1,0:T(8,128)(2,1)S(1)}, u32[]{:S(2)}, u32[]{:S(2)}) %collective-permute-start) | collective-permute-done | bytes 131104 | tf_op jit(solution)/shard_map/ppermute | solution.py:288
  14.8 0.0 copy-done
  14.8 0.0 copy-done.1
  14.8 3.7 %shard_map.46 = (f32[2048,128]{1,0:T(8,128)S(1)}, f32[2048,128]{1,0:T(8,128)S(1)}, f32[2048,128]{1,0:T(8,128)S(1)}, f32[2,8,128]{2,1,0:T(8,128)S(1)}) custom-call(s32[12]{0:T(128)S(1)} %copy-done.1, bf16[2048,128]{1,0:T(8,128)(2,1)S(1)} %bitcast.6, bf16[2,256,128]{2,1,0:T(8,128)(2,1)S(1)} %pad_maximum_fusion.1.own, ...), custom_call_target="tpu_custom_call" | custom-call | flops 1610612736 | bytes 16777216 | tf_op jit(solution)/shard_map/pallas_call | solution.py:295
  18.6 0.0 copy-start.2
  18.6 1.0 %copy-done.2 = f32[2048,128]{1,0:T(8,128)} copy-done((f32[2048,128]{1,0:T(8,128)}, f32[2048,128]{1,0:T(8,128)S(1)}, u32[]{:S(2)}) %copy-start.2) | copy-done | bytes 1048600
  19.6 0.0 copy-start.4
  19.6 1.0 %copy-done.4 = f32[2048,128]{1,0:T(8,128)} copy-done((f32[2048,128]{1,0:T(8,128)}, f32[2048,128]{1,0:T(8,128)S(1)}, u32[]{:S(2)}) %copy-start.4) | copy-done | bytes 1048600
  20.6 1.5 %all-to-all-done.kv = bf16[8,2,256,128]{3,2,1,0:T(8,128)(2,1)S(1)} async-done(((bf16[8,2,256,128]{3,2,1,0:T(8,128)(2,1)}), bf16[8,2,256,128]{3,2,1,0:T(8,128)(2,1)S(1)}, u32[]{:S(2)}, u32[]{:S(2)}) %all-to-all-start) | async-done | bytes 1048608 | tf_op jit(solution)/shard_map/all_to_all | solution.py:287
  22.0 3.0 %collective-permute-start.1 = (bf16[8,2,256,128]{3,2,1,0:T(8,128)(2,1)S(1)}, bf16[8,2,256,128]{3,2,1,0:T(8,128)(2,1)S(1)}, u32[]{:S(2)}, u32[]{:S(2)}) collective-permute-start(bf16[8,2,256,128]{3,2,1,0:T(8,128)(2,1)S(1)} %all-to-all-done.kv), channel_id=1, source_target_pairs={{0,8},{8,0},{16,24},{24,16},{32,40},{40,32},{48,56},{56,48},{64,72... | collective-permute-start | bytes 3145736 | tf_op jit(solution)/shard_map/ppermute | solution.py:307
  25.1 0.0 copy-start.3
  25.1 0.0 copy-start.5
  25.1 6.8 %shard_map.47 = (f32[2048,128]{1,0:T(8,128)S(1)}, f32[2048,128]{1,0:T(8,128)S(1)}, f32[2048,128]{1,0:T(8,128)S(1)}) custom-call(s32[12]{0:T(128)S(1)} %copy-done.1, bf16[2048,128]{1,0:T(8,128)(2,1)S(1)} %bitcast.7, bf16[8,2,256,128]{3,2,1,0:T(8,128)(2,1)S(1)} %all-to-all-done.kv, f32[2,8,128]{2,1,0:T(8,128)S(1)} %get-tuple-element.22.reach, ...), custom_call_target="tpu_custom_call" | custom-call | flops 3758096384 | bytes 16777216 | tf_op jit(solution)/shard_map/pallas_call | solution.py:308
  31.9 0.0 collective-permute-done.1.kv
  31.9 0.0 copy-done.3
  31.9 0.0 copy-done.5
  31.9 7.9 %shard_map.48 = bf16[2048,128]{1,0:T(8,128)(2,1)} custom-call(s32[12]{0:T(128)S(1)} %copy-done.1, bf16[2048,128]{1,0:T(8,128)(2,1)S(1)} %bitcast.8, bf16[8,2,256,128]{3,2,1,0:T(8,128)(2,1)S(1)} %collective-permute-done.1.kv, f32[2048,128]{1,0:T(8,128)S(1)} %get-tuple-element.23.near_best, f32[2048,128]{1,0:T(8,128)S(1)} %copy-done.3, ...), custom_call_target="tpu_custom_call" | custom-call | flops 3758096384 | bytes 16777216 | tf_op jit(solution)/shard_map/pallas_call | solution.py:319
  (1 shorter events, 0.0 us)
Async XLA Ops:
  2.1 9.5 %copy-start.6 = (bf16[256,1,128]{2,0,1:T(8,128)(2,1)S(1)}, bf16[256,1,128]{2,0,1:T(8,128)(2,1)}, u32[]{:S(2)}) copy-start(bf16[256,1,128]{2,0,1:T(8,128)(2,1)} %param.6) | copy-start | bytes 196612
  2.1 9.5 %copy-start.7 = (bf16[256,1,128]{2,0,1:T(8,128)(2,1)S(1)}, bf16[256,1,128]{2,0,1:T(8,128)(2,1)}, u32[]{:S(2)}) copy-start(bf16[256,1,128]{2,0,1:T(8,128)(2,1)} %param.5) | copy-start | bytes 196612
  2.1 12.8 %copy-start = (bf16[256,8,128]{2,1,0:T(8,128)(2,1)S(1)}, bf16[256,8,128]{2,1,0:T(8,128)(2,1)}, u32[]{:S(2)}) copy-start(bf16[256,8,128]{2,1,0:T(8,128)(2,1)} %param.4) | copy-start | bytes 1572868
  2.1 19.9 %all-to-all-start = ((bf16[8,2,256,128]{3,2,1,0:T(8,128)(2,1)}), bf16[8,2,256,128]{3,2,1,0:T(8,128)(2,1)S(1)}, u32[]{:S(2)}, u32[]{:S(2)}) async-start(bf16[8,2,256,128]{3,2,1,0:T(8,128)(2,1)} %broadcast_in_dim.2), calls=%async_computation | async-start | bytes 2097152 | tf_op jit(solution)/shard_map/all_to_all | solution.py:287
  11.6 3.3 %copy-start.1 = (s32[12]{0:T(128)S(1)}, s32[12]{0:T(128)}, u32[]{:S(2)}) copy-start(s32[12]{0:T(128)} %lengths.5) | copy-start | bytes 148
  11.6 3.2 %collective-permute-start = (bf16[2,256,128]{2,1,0:T(8,128)(2,1)S(1)}, bf16[2,256,128]{2,1,0:T(8,128)(2,1)S(1)}, u32[]{:S(2)}, u32[]{:S(2)}) collective-permute-start(bf16[2,256,128]{2,1,0:T(8,128)(2,1)S(1)} %pad_maximum_fusion.1.own), channel_id=1, source_target_pairs={{0,8},{8,0},{16,24},{24,16},{32,40},{40,32},{48,56},{56,48},{64,72... | collective-permute-start | bytes 393224 | tf_op jit(solution)/shard_map/ppermute | solution.py:288
  18.6 1.0 %copy-start.2 = (f32[2048,128]{1,0:T(8,128)}, f32[2048,128]{1,0:T(8,128)S(1)}, u32[]{:S(2)}) copy-start(f32[2048,128]{1,0:T(8,128)S(1)} %get-tuple-element.20.near_total) | copy-start | bytes 3145732
  19.6 1.0 %copy-start.4 = (f32[2048,128]{1,0:T(8,128)}, f32[2048,128]{1,0:T(8,128)S(1)}, u32[]{:S(2)}) copy-start(f32[2048,128]{1,0:T(8,128)S(1)} %get-tuple-element.21.near_acc) | copy-start | bytes 3145732
  22.0 9.9 %collective-permute-start.1 = (bf16[8,2,256,128]{3,2,1,0:T(8,128)(2,1)S(1)}, bf16[8,2,256,128]{3,2,1,0:T(8,128)(2,1)S(1)}, u32[]{:S(2)}, u32[]{:S(2)}) collective-permute-start(bf16[8,2,256,128]{3,2,1,0:T(8,128)(2,1)S(1)} %all-to-all-done.kv), channel_id=1, source_target_pairs={{0,8},{8,0},{16,24},{24,16},{32,40},{40,32},{48,56},{56,48},{64,72... | collective-permute-start | bytes 3145736 | tf_op jit(solution)/shard_map/ppermute | solution.py:307
  25.1 6.8 %copy-start.3 = (f32[2048,128]{1,0:T(8,128)S(1)}, f32[2048,128]{1,0:T(8,128)}, u32[]{:S(2)}) copy-start(f32[2048,128]{1,0:T(8,128)} %copy-done.2) | copy-start | bytes 3145732
  25.1 6.8 %copy-start.5 = (f32[2048,128]{1,0:T(8,128)S(1)}, f32[2048,128]{1,0:T(8,128)}, u32[]{:S(2)}) copy-start(f32[2048,128]{1,0:T(8,128)} %copy-done.4) | copy-start | bytes 3145732

commit v5 on v4

--- a/solution.py
+++ b/solution.py
@@ -10,6 +10,7 @@
 HEAD = 128
 CHUNK = 256
 BLOCK = 512
+PART = 256
 LOG2_SCALE = HEAD**-0.5 * 1.4426950408889634
 LOWEST = -1e30
 HIDDEN = 1e30
@@ -101,7 +102,17 @@
     reach[1] = jnp.broadcast_to(jnp.min(least, axis=0, keepdims=True), (8, HEAD))
 
 
-def fold_chunks(lengths, q, kv, reach, best, total, acc, here, there, mine):
+def bounded(kv, reach):
+    peak = jnp.zeros((8, HEAD), jnp.float32)
+    for i in range(kv.shape[0]):
+        size = jnp.abs(kv[i, 0].astype(jnp.float32))
+        peak = jnp.maximum(peak, jnp.max(size.reshape(CHUNK // 8, 8, HEAD), axis=0))
+    peak = jnp.max(peak, axis=0, keepdims=True)
+    size = jnp.sum(jnp.square(peak), axis=1, keepdims=True)
+    return jnp.max(jnp.sqrt(size * reach[0, :1]) * 1.01 - reach[1, :1]) < REACH
+
+
+def fold_chunks(lengths, q, kv, near, best, total, acc, here, there, mine):
     rows = q.shape[0]
     position, _, first_start, _ = place(lengths)
     core = lax.rem(position, 2)
@@ -168,23 +179,23 @@
 
         def score(r):
             return [
-                jnp.where(seen[i], scores(q[r : r + BLOCK, :], kv[tile + i, 0]), LOWEST)
+                jnp.where(seen[i], scores(q[r : r + PART, :], kv[tile + i, 0]), LOWEST)
                 for i in range(count)
             ]
 
         def add(r, low):
-            acc[r : r + BLOCK, :] += sum(
+            acc[r : r + PART, :] += sum(
                 jnp.dot(part, kv[tile + i, 1], preferred_element_type=jnp.float32)
                 for i, part in enumerate(low)
             )
 
         s = score(0)
         waiting = None
-        for r in range(0, rows, BLOCK):
-            later = score(r + BLOCK) if r + BLOCK < rows else None
+        for r in range(0, rows, PART):
+            later = score(r + PART) if r + PART < rows else None
             if waiting is not None:
                 add(*waiting)
-            rs = slice(r, r + BLOCK)
+            rs = slice(r, r + PART)
             base = best[rs, :] * LOG2_SCALE
             weights = [
                 [jnp.exp2(part * LOG2_SCALE - base) for part in split(block)] for block in s
@@ -196,15 +207,6 @@
 
     @pl.when(lo < hi)
     def _():
-        peak = jnp.zeros((8, HEAD), jnp.float32)
-        for i in range(kv.shape[0]):
-            size = jnp.abs(kv[i, 0].astype(jnp.float32))
-            peak = jnp.maximum(peak, jnp.max(size.reshape(CHUNK // 8, 8, HEAD), axis=0))
-        peak = jnp.max(peak, axis=0, keepdims=True)
-        size = jnp.sum(jnp.square(peak), axis=1, keepdims=True)
-        bound = jnp.sqrt(size * reach[0, :1]) * 1.01 - reach[1, :1]
-        near = jnp.max(bound) < REACH
-
         @pl.when(near)
         def _():
             count = hi - lo
@@ -237,10 +239,11 @@
 
 
 def middle_kernel(lengths, q, kv, reach, near_best, best, total, acc, here, there):
+    near = bounded(kv, reach)
     best[...] = near_best[...]
     total[...] = jnp.zeros(total.shape, jnp.float32)
     acc[...] = jnp.zeros(acc.shape, jnp.float32)
-    fold_chunks(lengths, q, kv, reach, best, total, acc, here, there, True)
+    fold_chunks(lengths, q, kv, near, best, total, acc, here, there, True)
 
 
 def last_kernel(
@@ -261,13 +264,14 @@
     here,
     there,
 ):
+    near = bounded(kv, reach)
     for r in range(0, out.shape[0], BLOCK):
         rs = slice(r, r + BLOCK)
         shrink = jnp.exp2((near_best[rs, :] - best_in[rs, :]) * LOG2_SCALE)
         best[rs, :] = best_in[rs, :]
         total[rs, :] = total_in[rs, :] + near_total[rs, :] * shrink
         acc[rs, :] = acc_in[rs, :] + near_acc[rs, :] * shrink
-    fold_chunks(lengths, q, kv, reach, best, total, acc, here, there, False)
+    fold_chunks(lengths, q, kv, near, best, total, acc, here, there, False)
     for r in range(0, out.shape[0], BLOCK):
         rs = slice(r, r + BLOCK)
         out[rs, :] = (acc[rs, :] / jnp.sum(total[rs, :], axis=1, keepdims=True)).astype(out.dtype)

time: 40 us -> 39.3 us (0.982)
  Pallas kernels: 18.4 us -> 17.4 us
    pallas_call x1, Pallas kernels: 6.8 us -> 5.75 us  [per_device(): pl.pallas_call(middle_kernel, out_shape=(wide, wide, wide), in_specs=[sme...]
  transfers between devices with their start and end apart: 3 -> 3, of which waited for: 2 -> 2; matrix products, arithmetic and copies ran while one was open for 0% -> 0% of each run, Pallas kernels for 26% -> 24%
where the time goes in v5:
time: 39.3 us; the launch traced here: 38.8 us
  Pallas kernels  17.4 us (44%)
  starting transfers between devices  14.4 us (37%)
  local copies, waits for them, and re-layouts  3.17 us (8%)
  waiting for transfers between devices  2.77 us (7%)
  other arithmetic  0.9 us (2%)
    all_to_all x1, starting transfers between devices, per_device(): mine = lax.all_to_all(spread, 'ctx', 0, 0, axis_index_groups=groups)  9.48 us
    pallas_call x1, Pallas kernels, per_device(): pl.pallas_call(last_kernel, out_shape=jax.ShapeDtypeStruct((rows, HEAD),...  7.95 us
    pallas_call x1, Pallas kernels, per_device(): pl.pallas_call(middle_kernel, out_shape=(wide, wide, wide), in_specs=[sme...  5.75 us
    pallas_call x1, Pallas kernels, per_device(): pl.pallas_call(local_kernel, out_shape=(wide, wide, wide, jax.ShapeDtypeS...  3.74 us
    ppermute x1, starting transfers between devices, per_device(): theirs = lax.ppermute(mine, 'ctx', swap)  3.04 us
    unnamed x16, local copies, waits for them, and re-layouts  1.99 us
    ppermute x1, starting transfers between devices, per_device(): partner = lax.ppermute(kv, 'ctx', swap)  1.92 us
    all_to_all x1, waiting for transfers between devices, per_device(): mine = lax.all_to_all(spread, 'ctx', 0, 0, axis_index_groups=groups)  1.46 us
  transfers between devices with their start and end apart: 3, of which 2 were waited for; matrix products, arithmetic and copies ran while one was open for 0% of the time, Pallas kernels for 24%

profile of v5, /device:TPU:6, one launch (start us, length us, event | category | flops | bytes accessed | tf_op | source)
XLA Modules:
  0.0 38.8 jit_solution(3537307542283905741)
XLA Ops:
  0.0 0.9 %pad_maximum_fusion = bf16[2,256,128]{2,1,0:T(8,128)(2,1)S(1)} fusion(bf16[1,256,128]{2,1,0:T(8,128)(2,1)} %bitcast.9, bf16[1,256,128]{2,1,0:T(8,128)(2,1)} %bitcast.11), kind=kLoop, calls=%fused_computation | loop fusion | flops 65536 | bytes 262144 | tf_op jit(solution)/shard_map/stack | solution.py:285
  0.9 1.2 %broadcast_in_dim.2 = bf16[8,2,256,128]{3,2,1,0:T(8,128)(2,1)} broadcast(bf16[2,256,128]{2,1,0:T(8,128)(2,1)S(1)} %pad_maximum_fusion), dimensions={1,2,3} | broadcast | bytes 1179648 | tf_op jit(solution)/shard_map/broadcast_in_dim | solution.py:284
  2.1 0.0 copy-start.6
  2.1 0.0 copy-start.7
  2.1 0.0 copy-start
  2.1 9.5 %all-to-all-start = ((bf16[8,2,256,128]{3,2,1,0:T(8,128)(2,1)}), bf16[8,2,256,128]{3,2,1,0:T(8,128)(2,1)S(1)}, u32[]{:S(2)}, u32[]{:S(2)}) async-start(bf16[8,2,256,128]{3,2,1,0:T(8,128)(2,1)} %broadcast_in_dim.2), calls=%async_computation | async-start | bytes 2097152 | tf_op jit(solution)/shard_map/all_to_all | solution.py:291
  11.5 0.0 copy-done.6
  11.5 0.0 copy-done.7
  11.6 0.0 copy-start.1
  11.6 1.9 %collective-permute-start = (bf16[2,256,128]{2,1,0:T(8,128)(2,1)S(1)}, bf16[2,256,128]{2,1,0:T(8,128)(2,1)S(1)}, u32[]{:S(2)}, u32[]{:S(2)}) collective-permute-start(bf16[2,256,128]{2,1,0:T(8,128)(2,1)S(1)} %pad_maximum_fusion.1.own), channel_id=1, source_target_pairs={{0,8},{8,0},{16,24},{24,16},{32,40},{40,32},{48,56},{56,48},{64,72... | collective-permute-start | bytes 393224 | tf_op jit(solution)/shard_map/ppermute | solution.py:292
  13.5 1.3 %collective-permute-done.partner = bf16[2,256,128]{2,1,0:T(8,128)(2,1)S(1)} collective-permute-done((bf16[2,256,128]{2,1,0:T(8,128)(2,1)S(1)}, bf16[2,256,128]{2,1,0:T(8,128)(2,1)S(1)}, u32[]{:S(2)}, u32[]{:S(2)}) %collective-permute-start) | collective-permute-done | bytes 131104 | tf_op jit(solution)/shard_map/ppermute | solution.py:292
  14.8 0.0 copy-done
  14.8 0.0 copy-done.1
  14.8 3.7 %shard_map.46 = (f32[2048,128]{1,0:T(8,128)S(1)}, f32[2048,128]{1,0:T(8,128)S(1)}, f32[2048,128]{1,0:T(8,128)S(1)}, f32[2,8,128]{2,1,0:T(8,128)S(1)}) custom-call(s32[12]{0:T(128)S(1)} %copy-done.1, bf16[2048,128]{1,0:T(8,128)(2,1)S(1)} %bitcast.6, bf16[2,256,128]{2,1,0:T(8,128)(2,1)S(1)} %pad_maximum_fusion.1.own, ...), custom_call_target="tpu_custom_call" | custom-call | flops 1610612736 | bytes 16777216 | tf_op jit(solution)/shard_map/pallas_call | solution.py:299
  18.6 0.0 copy-start.2
  18.6 1.0 %copy-done.2 = f32[2048,128]{1,0:T(8,128)} copy-done((f32[2048,128]{1,0:T(8,128)}, f32[2048,128]{1,0:T(8,128)S(1)}, u32[]{:S(2)}) %copy-start.2) | copy-done | bytes 1048600
  19.6 0.0 copy-start.4
  19.6 1.0 %copy-done.4 = f32[2048,128]{1,0:T(8,128)} copy-done((f32[2048,128]{1,0:T(8,128)}, f32[2048,128]{1,0:T(8,128)S(1)}, u32[]{:S(2)}) %copy-start.4) | copy-done | bytes 1048600
  20.6 1.5 %all-to-all-done.kv = bf16[8,2,256,128]{3,2,1,0:T(8,128)(2,1)S(1)} async-done(((bf16[8,2,256,128]{3,2,1,0:T(8,128)(2,1)}), bf16[8,2,256,128]{3,2,1,0:T(8,128)(2,1)S(1)}, u32[]{:S(2)}, u32[]{:S(2)}) %all-to-all-start) | async-done | bytes 1048608 | tf_op jit(solution)/shard_map/all_to_all | solution.py:291
  22.0 3.0 %collective-permute-start.1 = (bf16[8,2,256,128]{3,2,1,0:T(8,128)(2,1)S(1)}, bf16[8,2,256,128]{3,2,1,0:T(8,128)(2,1)S(1)}, u32[]{:S(2)}, u32[]{:S(2)}) collective-permute-start(bf16[8,2,256,128]{3,2,1,0:T(8,128)(2,1)S(1)} %all-to-all-done.kv), channel_id=1, source_target_pairs={{0,8},{8,0},{16,24},{24,16},{32,40},{40,32},{48,56},{56,48},{64,72... | collective-permute-start | bytes 3145736 | tf_op jit(solution)/shard_map/ppermute | solution.py:311
  25.1 0.0 copy-start.3
  25.1 0.0 copy-start.5
  25.1 5.8 %shard_map.47 = (f32[2048,128]{1,0:T(8,128)S(1)}, f32[2048,128]{1,0:T(8,128)S(1)}, f32[2048,128]{1,0:T(8,128)S(1)}) custom-call(s32[12]{0:T(128)S(1)} %copy-done.1, bf16[2048,128]{1,0:T(8,128)(2,1)S(1)} %bitcast.7, bf16[8,2,256,128]{3,2,1,0:T(8,128)(2,1)S(1)} %all-to-all-done.kv, f32[2,8,128]{2,1,0:T(8,128)S(1)} %get-tuple-element.22.reach, ...), custom_call_target="tpu_custom_call" | custom-call | flops 3758096384 | bytes 16777216 | tf_op jit(solution)/shard_map/pallas_call | solution.py:312
  30.8 0.0 collective-permute-done.1.kv
  30.8 0.0 copy-done.3
  30.9 0.0 copy-done.5
  30.9 7.9 %shard_map.48 = bf16[2048,128]{1,0:T(8,128)(2,1)} custom-call(s32[12]{0:T(128)S(1)} %copy-done.1, bf16[2048,128]{1,0:T(8,128)(2,1)S(1)} %bitcast.8, bf16[8,2,256,128]{3,2,1,0:T(8,128)(2,1)S(1)} %collective-permute-done.1.kv, f32[2048,128]{1,0:T(8,128)S(1)} %get-tuple-element.23.near_best, f32[2048,128]{1,0:T(8,128)S(1)} %copy-done.3, ...), custom_call_target="tpu_custom_call" | custom-call | flops 3758096384 | bytes 16777216 | tf_op jit(solution)/shard_map/pallas_call | solution.py:323
  (1 shorter events, 0.0 us)
Async XLA Ops:
  2.1 9.5 %copy-start.6 = (bf16[256,1,128]{2,0,1:T(8,128)(2,1)S(1)}, bf16[256,1,128]{2,0,1:T(8,128)(2,1)}, u32[]{:S(2)}) copy-start(bf16[256,1,128]{2,0,1:T(8,128)(2,1)} %param.6) | copy-start | bytes 196612
  2.1 9.5 %copy-start.7 = (bf16[256,1,128]{2,0,1:T(8,128)(2,1)S(1)}, bf16[256,1,128]{2,0,1:T(8,128)(2,1)}, u32[]{:S(2)}) copy-start(bf16[256,1,128]{2,0,1:T(8,128)(2,1)} %param.5) | copy-start | bytes 196612
  2.1 12.8 %copy-start = (bf16[256,8,128]{2,1,0:T(8,128)(2,1)S(1)}, bf16[256,8,128]{2,1,0:T(8,128)(2,1)}, u32[]{:S(2)}) copy-start(bf16[256,8,128]{2,1,0:T(8,128)(2,1)} %param.4) | copy-start | bytes 1572868
  2.1 19.9 %all-to-all-start = ((bf16[8,2,256,128]{3,2,1,0:T(8,128)(2,1)}), bf16[8,2,256,128]{3,2,1,0:T(8,128)(2,1)S(1)}, u32[]{:S(2)}, u32[]{:S(2)}) async-start(bf16[8,2,256,128]{3,2,1,0:T(8,128)(2,1)} %broadcast_in_dim.2), calls=%async_computation | async-start | bytes 2097152 | tf_op jit(solution)/shard_map/all_to_all | solution.py:291
  11.6 3.3 %copy-start.1 = (s32[12]{0:T(128)S(1)}, s32[12]{0:T(128)}, u32[]{:S(2)}) copy-start(s32[12]{0:T(128)} %lengths.5) | copy-start | bytes 148
  11.6 3.2 %collective-permute-start = (bf16[2,256,128]{2,1,0:T(8,128)(2,1)S(1)}, bf16[2,256,128]{2,1,0:T(8,128)(2,1)S(1)}, u32[]{:S(2)}, u32[]{:S(2)}) collective-permute-start(bf16[2,256,128]{2,1,0:T(8,128)(2,1)S(1)} %pad_maximum_fusion.1.own), channel_id=1, source_target_pairs={{0,8},{8,0},{16,24},{24,16},{32,40},{40,32},{48,56},{56,48},{64,72... | collective-permute-start | bytes 393224 | tf_op jit(solution)/shard_map/ppermute | solution.py:292
  18.6 1.0 %copy-start.2 = (f32[2048,128]{1,0:T(8,128)}, f32[2048,128]{1,0:T(8,128)S(1)}, u32[]{:S(2)}) copy-start(f32[2048,128]{1,0:T(8,128)S(1)} %get-tuple-element.20.near_total) | copy-start | bytes 3145732
  19.6 1.0 %copy-start.4 = (f32[2048,128]{1,0:T(8,128)}, f32[2048,128]{1,0:T(8,128)S(1)}, u32[]{:S(2)}) copy-start(f32[2048,128]{1,0:T(8,128)S(1)} %get-tuple-element.21.near_acc) | copy-start | bytes 3145732
  22.0 8.8 %collective-permute-start.1 = (bf16[8,2,256,128]{3,2,1,0:T(8,128)(2,1)S(1)}, bf16[8,2,256,128]{3,2,1,0:T(8,128)(2,1)S(1)}, u32[]{:S(2)}, u32[]{:S(2)}) collective-permute-start(bf16[8,2,256,128]{3,2,1,0:T(8,128)(2,1)S(1)} %all-to-all-done.kv), channel_id=1, source_target_pairs={{0,8},{8,0},{16,24},{24,16},{32,40},{40,32},{48,56},{56,48},{64,72... | collective-permute-start | bytes 3145736 | tf_op jit(solution)/shard_map/ppermute | solution.py:311
  25.1 5.8 %copy-start.3 = (f32[2048,128]{1,0:T(8,128)S(1)}, f32[2048,128]{1,0:T(8,128)}, u32[]{:S(2)}) copy-start(f32[2048,128]{1,0:T(8,128)} %copy-done.2) | copy-start | bytes 3145732
  25.1 5.8 %copy-start.5 = (f32[2048,128]{1,0:T(8,128)S(1)}, f32[2048,128]{1,0:T(8,128)}, u32[]{:S(2)}) copy-start(f32[2048,128]{1,0:T(8,128)} %copy-done.4) | copy-start | bytes 3145732

commit v6 on v5

--- a/solution.py
+++ b/solution.py
@@ -112,7 +112,7 @@
     return jnp.max(jnp.sqrt(size * reach[0, :1]) * 1.01 - reach[1, :1]) < REACH
 
 
-def fold_chunks(lengths, q, kv, near, best, total, acc, here, there, mine):
+def fold_chunks(lengths, q, kv, near, level, best, total, acc, here, there, mine):
     rows = q.shape[0]
     position, _, first_start, _ = place(lengths)
     core = lax.rem(position, 2)
@@ -196,7 +196,7 @@
             if waiting is not None:
                 add(*waiting)
             rs = slice(r, r + PART)
-            base = best[rs, :] * LOG2_SCALE
+            base = level[rs, :] * LOG2_SCALE
             weights = [
                 [jnp.exp2(part * LOG2_SCALE - base) for part in split(block)] for block in s
             ]
@@ -223,6 +223,7 @@
 
         @pl.when(jnp.logical_not(near))
         def _():
+            best[...] = level[...]
             stale = first_scores()
 
             def pair(i, stale):
@@ -243,7 +244,7 @@
     best[...] = near_best[...]
     total[...] = jnp.zeros(total.shape, jnp.float32)
     acc[...] = jnp.zeros(acc.shape, jnp.float32)
-    fold_chunks(lengths, q, kv, near, best, total, acc, here, there, True)
+    fold_chunks(lengths, q, kv, near, near_best, best, total, acc, here, there, True)
 
 
 def last_kernel(
@@ -263,18 +264,29 @@
     acc,
     here,
     there,
+    ready,
+    sems,
 ):
     near = bounded(kv, reach)
     for r in range(0, out.shape[0], BLOCK):
         rs = slice(r, r + BLOCK)
         shrink = jnp.exp2((near_best[rs, :] - best_in[rs, :]) * LOG2_SCALE)
-        best[rs, :] = best_in[rs, :]
         total[rs, :] = total_in[rs, :] + near_total[rs, :] * shrink
         acc[rs, :] = acc_in[rs, :] + near_acc[rs, :] * shrink
-    fold_chunks(lengths, q, kv, near, best, total, acc, here, there, False)
-    for r in range(0, out.shape[0], BLOCK):
+    fold_chunks(lengths, q, kv, near, best_in, best, total, acc, here, there, False)
+    copies = []
+    for i, r in enumerate(range(0, out.shape[0], BLOCK)):
         rs = slice(r, r + BLOCK)
-        out[rs, :] = (acc[rs, :] / jnp.sum(total[rs, :], axis=1, keepdims=True)).astype(out.dtype)
+        mixed = acc[rs, :] / jnp.sum(total[rs, :], axis=1, keepdims=True)
+        ready[rs, :] = mixed.astype(out.dtype)
+        copies.append(
+            pltpu.make_async_copy(
+                ready.at[pl.ds(r, BLOCK), :], out.at[pl.ds(r, BLOCK), :], sems.at[i]
+            )
+        )
+        copies[-1].start()
+    for copy in copies:
+        copy.wait()
 
 
 def per_device(queries, keys, values, doc_lengths):
@@ -324,8 +336,10 @@
         last_kernel,
         out_shape=jax.ShapeDtypeStruct((rows, HEAD), jnp.bfloat16),
         in_specs=[smem] + [vmem] * 9,
-        out_specs=vmem,
-        scratch_shapes=[pltpu.VMEM((rows, HEAD), jnp.float32)] * 3 + holds,
+        out_specs=pl.BlockSpec(memory_space=pl.ANY),
+        scratch_shapes=[pltpu.VMEM((rows, HEAD), jnp.float32)] * 3
+        + holds
+        + [pltpu.VMEM((rows, HEAD), jnp.bfloat16), pltpu.SemaphoreType.DMA((rows // BLOCK,))],
         compiler_params=params,
         cost_estimate=pl.CostEstimate(
             flops=14 * rows * CHUNK * HEAD * 4, bytes_accessed=2**24, transcendentals=0

time: 39.3 us -> 39.1 us (level)
  transfers between devices with their start and end apart: 3 -> 3, of which waited for: 2 -> 2; matrix products, arithmetic and copies ran while one was open for 0% -> 0% of each run, Pallas kernels for 24% -> 25%
where the time goes in v6:
time: 39.1 us; the launch traced here: 38.7 us
  Pallas kernels  17.3 us (44%)
  starting transfers between devices  14.4 us (37%)
  local copies, waits for them, and re-layouts  3.17 us (8%)
  waiting for transfers between devices  2.77 us (7%)
  other arithmetic  0.9 us (2%)
    all_to_all x1, starting transfers between devices, per_device(): mine = lax.all_to_all(spread, 'ctx', 0, 0, axis_index_groups=groups)  9.48 us
    pallas_call x1, Pallas kernels, per_device(): pl.pallas_call(last_kernel, out_shape=jax.ShapeDtypeStruct((rows, HEAD),...  7.81 us
    pallas_call x1, Pallas kernels, per_device(): pl.pallas_call(middle_kernel, out_shape=(wide, wide, wide), in_specs=[sme...  5.76 us
    pallas_call x1, Pallas kernels, per_device(): pl.pallas_call(local_kernel, out_shape=(wide, wide, wide, jax.ShapeDtypeS...  3.74 us
    ppermute x1, starting transfers between devices, per_device(): theirs = lax.ppermute(mine, 'ctx', swap)  3.04 us
    unnamed x16, local copies, waits for them, and re-layouts  1.99 us
    ppermute x1, starting transfers between devices, per_device(): partner = lax.ppermute(kv, 'ctx', swap)  1.92 us
    all_to_all x1, waiting for transfers between devices, per_device(): mine = lax.all_to_all(spread, 'ctx', 0, 0, axis_index_groups=groups)  1.46 us
  transfers between devices with their start and end apart: 3, of which 2 were waited for; matrix products, arithmetic and copies ran while one was open for 0% of the time, Pallas kernels for 25%

profile of v6, /device:TPU:6, one launch (start us, length us, event | category | flops | bytes accessed | tf_op | source)
XLA Modules:
  0.0 38.7 jit_solution(13844355238846879258)
XLA Ops:
  0.0 0.9 %pad_maximum_fusion = bf16[2,256,128]{2,1,0:T(8,128)(2,1)S(1)} fusion(bf16[1,256,128]{2,1,0:T(8,128)(2,1)} %bitcast.9, bf16[1,256,128]{2,1,0:T(8,128)(2,1)} %bitcast.11), kind=kLoop, calls=%fused_computation | loop fusion | flops 65536 | bytes 262144 | tf_op jit(solution)/shard_map/stack | solution.py:297
  0.9 1.2 %broadcast_in_dim.2 = bf16[8,2,256,128]{3,2,1,0:T(8,128)(2,1)} broadcast(bf16[2,256,128]{2,1,0:T(8,128)(2,1)S(1)} %pad_maximum_fusion), dimensions={1,2,3} | broadcast | bytes 1179648 | tf_op jit(solution)/shard_map/broadcast_in_dim | solution.py:296
  2.1 0.0 copy-start.6
  2.1 0.0 copy-start.7
  2.1 0.0 copy-start
  2.1 9.5 %all-to-all-start = ((bf16[8,2,256,128]{3,2,1,0:T(8,128)(2,1)}), bf16[8,2,256,128]{3,2,1,0:T(8,128)(2,1)S(1)}, u32[]{:S(2)}, u32[]{:S(2)}) async-start(bf16[8,2,256,128]{3,2,1,0:T(8,128)(2,1)} %broadcast_in_dim.2), calls=%async_computation | async-start | bytes 2097152 | tf_op jit(solution)/shard_map/all_to_all | solution.py:303
  11.5 0.0 copy-done.6
  11.5 0.0 copy-done.7
  11.6 0.0 copy-start.1
  11.6 1.9 %collective-permute-start = (bf16[2,256,128]{2,1,0:T(8,128)(2,1)S(1)}, bf16[2,256,128]{2,1,0:T(8,128)(2,1)S(1)}, u32[]{:S(2)}, u32[]{:S(2)}) collective-permute-start(bf16[2,256,128]{2,1,0:T(8,128)(2,1)S(1)} %pad_maximum_fusion.1.own), channel_id=1, source_target_pairs={{0,8},{8,0},{16,24},{24,16},{32,40},{40,32},{48,56},{56,48},{64,72... | collective-permute-start | bytes 393224 | tf_op jit(solution)/shard_map/ppermute | solution.py:304
  13.5 1.3 %collective-permute-done.partner = bf16[2,256,128]{2,1,0:T(8,128)(2,1)S(1)} collective-permute-done((bf16[2,256,128]{2,1,0:T(8,128)(2,1)S(1)}, bf16[2,256,128]{2,1,0:T(8,128)(2,1)S(1)}, u32[]{:S(2)}, u32[]{:S(2)}) %collective-permute-start) | collective-permute-done | bytes 131104 | tf_op jit(solution)/shard_map/ppermute | solution.py:304
  14.8 0.0 copy-done
  14.8 0.0 copy-done.1
  14.8 3.7 %shard_map.46 = (f32[2048,128]{1,0:T(8,128)S(1)}, f32[2048,128]{1,0:T(8,128)S(1)}, f32[2048,128]{1,0:T(8,128)S(1)}, f32[2,8,128]{2,1,0:T(8,128)S(1)}) custom-call(s32[12]{0:T(128)S(1)} %copy-done.1, bf16[2048,128]{1,0:T(8,128)(2,1)S(1)} %bitcast.6, bf16[2,256,128]{2,1,0:T(8,128)(2,1)S(1)} %pad_maximum_fusion.1.own, ...), custom_call_target="tpu_custom_call" | custom-call | flops 1610612736 | bytes 16777216 | tf_op jit(solution)/shard_map/pallas_call | solution.py:311
  18.6 0.0 copy-start.2
  18.6 1.0 %copy-done.2 = f32[2048,128]{1,0:T(8,128)} copy-done((f32[2048,128]{1,0:T(8,128)}, f32[2048,128]{1,0:T(8,128)S(1)}, u32[]{:S(2)}) %copy-start.2) | copy-done | bytes 1048600
  19.6 0.0 copy-start.4
  19.6 1.0 %copy-done.4 = f32[2048,128]{1,0:T(8,128)} copy-done((f32[2048,128]{1,0:T(8,128)}, f32[2048,128]{1,0:T(8,128)S(1)}, u32[]{:S(2)}) %copy-start.4) | copy-done | bytes 1048600
  20.6 1.5 %all-to-all-done.kv = bf16[8,2,256,128]{3,2,1,0:T(8,128)(2,1)S(1)} async-done(((bf16[8,2,256,128]{3,2,1,0:T(8,128)(2,1)}), bf16[8,2,256,128]{3,2,1,0:T(8,128)(2,1)S(1)}, u32[]{:S(2)}, u32[]{:S(2)}) %all-to-all-start) | async-done | bytes 1048608 | tf_op jit(solution)/shard_map/all_to_all | solution.py:303
  22.0 3.0 %collective-permute-start.1 = (bf16[8,2,256,128]{3,2,1,0:T(8,128)(2,1)S(1)}, bf16[8,2,256,128]{3,2,1,0:T(8,128)(2,1)S(1)}, u32[]{:S(2)}, u32[]{:S(2)}) collective-permute-start(bf16[8,2,256,128]{3,2,1,0:T(8,128)(2,1)S(1)} %all-to-all-done.kv), channel_id=1, source_target_pairs={{0,8},{8,0},{16,24},{24,16},{32,40},{40,32},{48,56},{56,48},{64,72... | collective-permute-start | bytes 3145736 | tf_op jit(solution)/shard_map/ppermute | solution.py:323
  25.1 0.0 copy-start.3
  25.1 0.0 copy-start.5
  25.1 5.8 %shard_map.47 = (f32[2048,128]{1,0:T(8,128)S(1)}, f32[2048,128]{1,0:T(8,128)S(1)}, f32[2048,128]{1,0:T(8,128)S(1)}) custom-call(s32[12]{0:T(128)S(1)} %copy-done.1, bf16[2048,128]{1,0:T(8,128)(2,1)S(1)} %bitcast.7, bf16[8,2,256,128]{3,2,1,0:T(8,128)(2,1)S(1)} %all-to-all-done.kv, f32[2,8,128]{2,1,0:T(8,128)S(1)} %get-tuple-element.22.reach, ...), custom_call_target="tpu_custom_call" | custom-call | flops 3758096384 | bytes 16777216 | tf_op jit(solution)/shard_map/pallas_call | solution.py:324
  30.8 0.0 collective-permute-done.1.kv
  30.9 0.0 copy-done.3
  30.9 0.0 copy-done.5
  30.9 7.8 %shard_map.48 = bf16[2048,128]{1,0:T(8,128)(2,1)} custom-call(s32[12]{0:T(128)S(1)} %copy-done.1, bf16[2048,128]{1,0:T(8,128)(2,1)S(1)} %bitcast.8, bf16[8,2,256,128]{3,2,1,0:T(8,128)(2,1)S(1)} %collective-permute-done.1.kv, f32[2048,128]{1,0:T(8,128)S(1)} %get-tuple-element.23.near_best, f32[2048,128]{1,0:T(8,128)S(1)} %copy-done.3, ...), custom_call_target="tpu_custom_call" | custom-call | flops 3758096384 | bytes 16777216 | tf_op jit(solution)/shard_map/pallas_call | solution.py:335
  (1 shorter events, 0.0 us)
Async XLA Ops:
  2.1 9.5 %copy-start.6 = (bf16[256,1,128]{2,0,1:T(8,128)(2,1)S(1)}, bf16[256,1,128]{2,0,1:T(8,128)(2,1)}, u32[]{:S(2)}) copy-start(bf16[256,1,128]{2,0,1:T(8,128)(2,1)} %param.6) | copy-start | bytes 196612
  2.1 9.5 %copy-start.7 = (bf16[256,1,128]{2,0,1:T(8,128)(2,1)S(1)}, bf16[256,1,128]{2,0,1:T(8,128)(2,1)}, u32[]{:S(2)}) copy-start(bf16[256,1,128]{2,0,1:T(8,128)(2,1)} %param.5) | copy-start | bytes 196612
  2.1 12.8 %copy-start = (bf16[256,8,128]{2,1,0:T(8,128)(2,1)S(1)}, bf16[256,8,128]{2,1,0:T(8,128)(2,1)}, u32[]{:S(2)}) copy-start(bf16[256,8,128]{2,1,0:T(8,128)(2,1)} %param.4) | copy-start | bytes 1572868
  2.1 19.9 %all-to-all-start = ((bf16[8,2,256,128]{3,2,1,0:T(8,128)(2,1)}), bf16[8,2,256,128]{3,2,1,0:T(8,128)(2,1)S(1)}, u32[]{:S(2)}, u32[]{:S(2)}) async-start(bf16[8,2,256,128]{3,2,1,0:T(8,128)(2,1)} %broadcast_in_dim.2), calls=%async_computation | async-start | bytes 2097152 | tf_op jit(solution)/shard_map/all_to_all | solution.py:303
  11.6 3.3 %copy-start.1 = (s32[12]{0:T(128)S(1)}, s32[12]{0:T(128)}, u32[]{:S(2)}) copy-start(s32[12]{0:T(128)} %lengths.5) | copy-start | bytes 148
  11.6 3.2 %collective-permute-start = (bf16[2,256,128]{2,1,0:T(8,128)(2,1)S(1)}, bf16[2,256,128]{2,1,0:T(8,128)(2,1)S(1)}, u32[]{:S(2)}, u32[]{:S(2)}) collective-permute-start(bf16[2,256,128]{2,1,0:T(8,128)(2,1)S(1)} %pad_maximum_fusion.1.own), channel_id=1, source_target_pairs={{0,8},{8,0},{16,24},{24,16},{32,40},{40,32},{48,56},{56,48},{64,72... | collective-permute-start | bytes 393224 | tf_op jit(solution)/shard_map/ppermute | solution.py:304
  18.6 1.0 %copy-start.2 = (f32[2048,128]{1,0:T(8,128)}, f32[2048,128]{1,0:T(8,128)S(1)}, u32[]{:S(2)}) copy-start(f32[2048,128]{1,0:T(8,128)S(1)} %get-tuple-element.20.near_total) | copy-start | bytes 3145732
  19.6 1.0 %copy-start.4 = (f32[2048,128]{1,0:T(8,128)}, f32[2048,128]{1,0:T(8,128)S(1)}, u32[]{:S(2)}) copy-start(f32[2048,128]{1,0:T(8,128)S(1)} %get-tuple-element.21.near_acc) | copy-start | bytes 3145732
  22.0 8.8 %collective-permute-start.1 = (bf16[8,2,256,128]{3,2,1,0:T(8,128)(2,1)S(1)}, bf16[8,2,256,128]{3,2,1,0:T(8,128)(2,1)S(1)}, u32[]{:S(2)}, u32[]{:S(2)}) collective-permute-start(bf16[8,2,256,128]{3,2,1,0:T(8,128)(2,1)S(1)} %all-to-all-done.kv), channel_id=1, source_target_pairs={{0,8},{8,0},{16,24},{24,16},{32,40},{40,32},{48,56},{56,48},{64,72... | collective-permute-start | bytes 3145736 | tf_op jit(solution)/shard_map/ppermute | solution.py:323
  25.1 5.8 %copy-start.3 = (f32[2048,128]{1,0:T(8,128)S(1)}, f32[2048,128]{1,0:T(8,128)}, u32[]{:S(2)}) copy-start(f32[2048,128]{1,0:T(8,128)} %copy-done.2) | copy-start | bytes 3145732
  25.1 5.8 %copy-start.5 = (f32[2048,128]{1,0:T(8,128)S(1)}, f32[2048,128]{1,0:T(8,128)}, u32[]{:S(2)}) copy-start(f32[2048,128]{1,0:T(8,128)} %copy-done.4) | copy-start | bytes 3145732
